TPU v7x, 32 devices: a whole 2x2x4 slice. The times are simulated.
32 devices in a mesh: dp: 4 (over z), fsdp: 8 (over y, x, core).
Axes of the slice: x: 2, y: 2, z: 4, core: 2. Of those that a mesh axis runs over, the one named last changes fastest.
Arguments:
- tokens: bfloat16 [138752, 768], P(('dp', 'fsdp')), may hold values from -6 to 6
- keep_slots: int32 [256, 268], P(('dp', 'fsdp')), may hold values from 0 to 541, as said below
- cotangent: bfloat16 [138752, 768], P(('dp', 'fsdp')), may hold values from -6 to 6
- project_in: float32 [768, 2304], P(('dp', 'fsdp')), may hold values from -0.21875 to 0.21875
- project_out: float32 [768, 768], P(('dp', 'fsdp')), may hold values from -0.625 to 0.625
- expand: float32 [768, 3072], P(('dp', 'fsdp')), may hold values from -0.21875 to 0.21875
- contract: float32 [3072, 768], P(('dp', 'fsdp')), may hold values from -0.109375 to 0.109375
- vectors: float32 [13, 768], P(None, ('dp', 'fsdp')), may hold values from -1.5 to 4.5
- first_in: float32 [768, 2304], P(('dp', 'fsdp')), may hold values from -0.3 to 0.3
- first_out: float32 [768, 768], P(('dp', 'fsdp')), may hold values from -0.3 to 0.3
- first_expand: float32 [768, 3072], P(('dp', 'fsdp')), may hold values from -0.3 to 0.3
- first_contract: float32 [3072, 768], P(('dp', 'fsdp')), may hold values from -0.3 to 0.3
- first_vectors: float32 [13, 768], P(None, ('dp', 'fsdp')), may hold values from -0.3 to 0.3
- second_in: float32 [768, 2304], P(('dp', 'fsdp')), may hold values from 0.0025 to 0.01
- second_out: float32 [768, 768], P(('dp', 'fsdp')), may hold values from 0.0025 to 0.01
- second_expand: float32 [768, 3072], P(('dp', 'fsdp')), may hold values from 0.0025 to 0.01
- second_contract: float32 [3072, 768], P(('dp', 'fsdp')), may hold values from 0.0025 to 0.01
- second_vectors: float32 [13, 768], P(None, ('dp', 'fsdp')), may hold values from 0.0025 to 0.01
Outputs:
- activations: bfloat16 [138752, 768], P(('dp', 'fsdp'))
- input_grad: bfloat16 [138752, 768], P(('dp', 'fsdp'))
- grad_norm: float32 [1], replicated
- momentum_in: float32 [768, 2304], P(('dp', 'fsdp'))
- momentum_out: float32 [768, 768], P(('dp', 'fsdp'))
- momentum_expand: float32 [768, 3072], P(('dp', 'fsdp'))
- momentum_contract: float32 [3072, 768], P(('dp', 'fsdp'))
- momentum_vectors: float32 [13, 768], P(None, ('dp', 'fsdp'))
- variance_in: float32 [768, 2304], P(('dp', 'fsdp'))
- variance_out: float32 [768, 768], P(('dp', 'fsdp'))
- variance_expand: float32 [768, 3072], P(('dp', 'fsdp'))
- variance_contract: float32 [3072, 768], P(('dp', 'fsdp'))
- variance_vectors: float32 [13, 768], P(None, ('dp', 'fsdp'))
- updated_in: float32 [768, 2304], P(('dp', 'fsdp'))
- updated_out: float32 [768, 768], P(('dp', 'fsdp'))
- updated_expand: float32 [768, 3072], P(('dp', 'fsdp'))
- updated_contract: float32 [3072, 768], P(('dp', 'fsdp'))
- updated_vectors: float32 [13, 768], P(None, ('dp', 'fsdp'))
- copy_in: bfloat16 [768, 2304], P(('dp', 'fsdp'))
- copy_out: bfloat16 [768, 768], P(('dp', 'fsdp'))
- copy_expand: bfloat16 [768, 3072], P(('dp', 'fsdp'))
- copy_contract: bfloat16 [3072, 768], P(('dp', 'fsdp'))
- copy_vectors: bfloat16 [13, 768], P(None, ('dp', 'fsdp'))
Inputs may be any that keep to these rules, and one draw needn't show every extreme that they name: `keep_slots`: row i lists the kept positions of image i: slots 0 to 97 hold distinct positions of its first global crop (positions 0 to 196) in ascending order, the next 98 slots distinct positions of the second global crop (the next 197 positions) in ascending order, then 18 slots for each of the four local crops of 37 positions that follow, likewise.
All inputs are finite; a program needn't handle non-finite values.
Results may differ from a plain program's by a relative error of at most 0.012.
The roundings to bfloat16 on the way count: a program that leaves them out, or rounds other values in their place, can miss the bound.
Values may be sent and summed in bfloat16 or wider, within the bound.
No kernel may reach another device: no remote copies, remote signals or barrier semaphores. Data moves between devices by JAX's collectives and lax.ppermute only.
A program may use at most 320 MiB of HBM per device.

v0:
```python
import math

import jax
import jax.numpy as jnp
from jax import lax
from jax.sharding import PartitionSpec as P

D = 768
HEADS = 12
HEAD_DIM = 64
KEEP_GLOBAL = 98
KEEP_LOCAL = 18
KEEP = 268
PARAMS = 7087872
STEP = 5


norm_eps = 1e-06
clip_share = 0.05
matrix_rate = 0.04
vector_rate = 0.3
matrix_decay = 0.05
first_beta = 0.5
second_beta = 0.5
adam_eps = 1e-08


def layer_norm(values, gain, shift):
    centred = values - jnp.mean(values, axis=-1, keepdims=True)
    spread = jnp.mean(centred * centred, axis=-1, keepdims=True)
    return centred * lax.rsqrt(spread + norm_eps) * gain + shift


def exact_gelu(values):
    return jax.nn.gelu(values, approximate=False)


def outer(left, right):
    return lax.dot_general(
        left, right, (((0,), (0,)), ((), ())), preferred_element_type=jnp.float32
    )


def inner(left, right):
    return lax.dot_general(
        left, right, (((1,), (1,)), ((), ())), preferred_element_type=jnp.float32
    )


def to_crops(flat, count):
    shaped = flat.reshape(count, KEEP, HEADS, HEAD_DIM)
    wide = shaped[:, : 2 * KEEP_GLOBAL].reshape(count * 2, KEEP_GLOBAL, HEADS, HEAD_DIM)
    narrow = shaped[:, 2 * KEEP_GLOBAL :].reshape(count * 4, KEEP_LOCAL, HEADS, HEAD_DIM)
    return (wide, narrow)


def from_crops(wide, narrow, count):
    joined = jnp.concatenate(
        [wide.reshape(count, 2 * KEEP_GLOBAL, D), narrow.reshape(count, 4 * KEEP_LOCAL, D)], axis=1
    )
    return joined.reshape(count * KEEP, D)


def crop_forward(query, key_rows, value):
    scores = jnp.einsum(
        "cqhe,ckhe->chqk", query, key_rows, preferred_element_type=jnp.float32
    ) * HEAD_DIM ** (-0.5)
    peak = jnp.max(scores, axis=-1, keepdims=True)
    shifted = jnp.exp(scores - peak)
    totals = jnp.sum(shifted, axis=-1, keepdims=True)
    probs_low = (shifted / totals).astype(jnp.bfloat16)
    result = jnp.einsum("chqk,ckhe->cqhe", probs_low, value, preferred_element_type=jnp.float32)
    return (result, peak + jnp.log(totals))


def crop_backward(query, key_rows, value, log_total, grad_out):
    factor = HEAD_DIM ** (-0.5)
    scores = (
        jnp.einsum("cqhe,ckhe->chqk", query, key_rows, preferred_element_type=jnp.float32) * factor
    )
    probs = jnp.exp(scores - log_total)
    grad_probs = jnp.einsum("cqhe,ckhe->chqk", grad_out, value, preferred_element_type=jnp.float32)
    weighted = jnp.sum(probs * grad_probs, axis=-1, keepdims=True)
    grad_scores = (probs * (grad_probs - weighted)).astype(jnp.bfloat16)
    grad_query = (
        jnp.einsum("chqk,ckhe->cqhe", grad_scores, key_rows, preferred_element_type=jnp.float32)
        * factor
    )
    grad_key = (
        jnp.einsum("chqk,cqhe->ckhe", grad_scores, query, preferred_element_type=jnp.float32)
        * factor
    )
    grad_value = jnp.einsum(
        "chqk,cqhe->ckhe", probs.astype(jnp.bfloat16), grad_out, preferred_element_type=jnp.float32
    )
    return (grad_query, grad_key, grad_value)


def adam_update(master, grad, first, second, rate, decay):
    first_new = first_beta * first + (1.0 - first_beta) * grad
    second_new = second_beta * second + (1.0 - second_beta) * grad * grad
    first_hat = first_new / (1.0 - first_beta**STEP)
    second_hat = second_new / (1.0 - second_beta**STEP)
    updated = master - rate * (first_hat / (jnp.sqrt(second_hat) + adam_eps) + decay * master)
    return (first_new, second_new, updated)


def on_device(
    tokens,
    keep_slots,
    cotangent,
    project_in,
    project_out,
    expand,
    contract,
    vectors,
    first_in,
    first_out,
    first_expand,
    first_contract,
    first_vectors,
    second_in,
    second_out,
    second_expand,
    second_contract,
    second_vectors,
):
    full = (
        lax.all_gather(project_in.astype(jnp.bfloat16), ("dp", "fsdp"), axis=0, tiled=True),
        lax.all_gather(project_out.astype(jnp.bfloat16), ("dp", "fsdp"), axis=0, tiled=True),
        lax.all_gather(expand.astype(jnp.bfloat16), ("dp", "fsdp"), axis=0, tiled=True),
        lax.all_gather(contract.astype(jnp.bfloat16), ("dp", "fsdp"), axis=0, tiled=True),
        lax.all_gather(vectors.astype(jnp.bfloat16), ("dp", "fsdp"), axis=1, tiled=True),
    )
    count = keep_slots.shape[0]
    image_tokens = tokens.shape[0] // count
    rows = (jnp.arange(count, dtype=jnp.int32)[:, None] * image_tokens + keep_slots).reshape(-1)
    picked = tokens[rows]
    picked_wide = picked.astype(jnp.float32)
    params = full[4].astype(jnp.float32)
    routed = jnp.dot(picked, full[4][8], preferred_element_type=jnp.float32)
    normed_one, pull_one = jax.vjp(layer_norm, picked_wide, params[0], params[1])
    normed_low = normed_one.astype(jnp.bfloat16)
    in_bias = jnp.concatenate([params[2], jnp.zeros((D,), jnp.float32), params[3]])
    mixed = (jnp.dot(normed_low, full[0], preferred_element_type=jnp.float32) + in_bias).astype(
        jnp.bfloat16
    )
    wide_q, narrow_q = to_crops(mixed[:, :D], count)
    wide_k, narrow_k = to_crops(mixed[:, D : 2 * D], count)
    wide_v, narrow_v = to_crops(mixed[:, 2 * D :], count)
    wide_out, wide_log = crop_forward(wide_q, wide_k, wide_v)
    narrow_out, narrow_log = crop_forward(narrow_q, narrow_k, narrow_v)
    heads_out = from_crops(wide_out, narrow_out, count).astype(jnp.bfloat16)
    attended = jnp.dot(heads_out, full[1], preferred_element_type=jnp.float32) + params[4]
    residual = picked_wide + attended
    normed_two, pull_two = jax.vjp(layer_norm, residual, params[5], params[6])
    normed_two_low = normed_two.astype(jnp.bfloat16)
    before = jnp.dot(normed_two_low, full[2], preferred_element_type=jnp.float32) + params[
        9:
    ].reshape(-1)
    active, pull_gelu = jax.vjp(exact_gelu, before)
    active_low = active.astype(jnp.bfloat16)
    mlp_out = jnp.dot(active_low, full[3], preferred_element_type=jnp.float32) + params[7]
    branch = attended + mlp_out
    activations = (
        tokens.astype(jnp.float32).at[rows].add(branch * routed[:, None]).astype(jnp.bfloat16)
    )
    back = (
        lax.all_gather(project_in.astype(jnp.bfloat16), ("dp", "fsdp"), axis=0, tiled=True),
        lax.all_gather(project_out.astype(jnp.bfloat16), ("dp", "fsdp"), axis=0, tiled=True),
        lax.all_gather(expand.astype(jnp.bfloat16), ("dp", "fsdp"), axis=0, tiled=True),
        lax.all_gather(contract.astype(jnp.bfloat16), ("dp", "fsdp"), axis=0, tiled=True),
        lax.all_gather(vectors.astype(jnp.bfloat16), ("dp", "fsdp"), axis=1, tiled=True),
    )
    grad_rows = cotangent[rows].astype(jnp.float32)
    grad_routed = jnp.sum(grad_rows * branch, axis=-1)
    grad_branch = grad_rows * routed[:, None]
    grad_mlp = grad_branch.astype(jnp.bfloat16)
    grad_contract = outer(active_low, grad_mlp)
    (grad_before,) = pull_gelu(inner(grad_mlp, back[3]))
    grad_before_low = grad_before.astype(jnp.bfloat16)
    grad_expand = outer(normed_two_low, grad_before_low)
    grad_residual, grad_gain_two, grad_shift_two = pull_two(inner(grad_before_low, back[2]))
    grad_attended = (grad_branch + grad_residual).astype(jnp.bfloat16)
    grad_project_out = outer(heads_out, grad_attended)
    grad_heads = inner(grad_attended, back[1]).astype(jnp.bfloat16)
    wide_grad, narrow_grad = to_crops(grad_heads, count)
    wide_dq, wide_dk, wide_dv = crop_backward(wide_q, wide_k, wide_v, wide_log, wide_grad)
    narrow_dq, narrow_dk, narrow_dv = crop_backward(
        narrow_q, narrow_k, narrow_v, narrow_log, narrow_grad
    )
    grad_mixed = jnp.concatenate(
        [
            from_crops(wide_dq, narrow_dq, count),
            from_crops(wide_dk, narrow_dk, count),
            from_crops(wide_dv, narrow_dv, count),
        ],
        axis=1,
    ).astype(jnp.bfloat16)
    grad_project_in = outer(normed_low, grad_mixed)
    grad_picked_norm, grad_gain_one, grad_shift_one = pull_one(inner(grad_mixed, back[0]))
    grad_router = jnp.dot(grad_routed, picked_wide, precision=lax.Precision.HIGHEST)
    grad_picked = grad_picked_norm + grad_residual + grad_routed[:, None] * params[8]
    input_grad = cotangent.astype(jnp.float32).at[rows].add(grad_picked).astype(jnp.bfloat16)
    mixed_sums = jnp.sum(grad_mixed.astype(jnp.float32), axis=0)
    grad_vectors = jnp.concatenate(
        [
            jnp.stack(
                [
                    grad_gain_one,
                    grad_shift_one,
                    mixed_sums[:D],
                    mixed_sums[2 * D :],
                    jnp.sum(grad_attended.astype(jnp.float32), axis=0),
                    grad_gain_two,
                    grad_shift_two,
                    jnp.sum(grad_mlp.astype(jnp.float32), axis=0),
                    grad_router,
                ]
            ),
            jnp.sum(grad_before_low.astype(jnp.float32), axis=0).reshape(-1, D),
        ],
        axis=0,
    )
    summed = (
        lax.psum_scatter(grad_project_in, ("dp", "fsdp"), scatter_dimension=0, tiled=True),
        lax.psum_scatter(grad_project_out, ("dp", "fsdp"), scatter_dimension=0, tiled=True),
        lax.psum_scatter(grad_expand, ("dp", "fsdp"), scatter_dimension=0, tiled=True),
        lax.psum_scatter(grad_contract, ("dp", "fsdp"), scatter_dimension=0, tiled=True),
        lax.psum_scatter(grad_vectors, ("dp", "fsdp"), scatter_dimension=1, tiled=True),
    )
    local_squares = jnp.sum(summed[0] * summed[0])
    for piece in summed[1:]:
        local_squares = local_squares + jnp.sum(piece * piece)
    total_squares = lax.psum(local_squares, ("dp", "fsdp"))
    grad_norm = jnp.sqrt(total_squares)
    factor = jnp.minimum(1.0, clip_share * math.sqrt(PARAMS) / (grad_norm + 1e-06))
    masters = (project_in, project_out, expand, contract, vectors)
    firsts = (first_in, first_out, first_expand, first_contract, first_vectors)
    seconds = (second_in, second_out, second_expand, second_contract, second_vectors)
    rates = (matrix_rate, matrix_rate, matrix_rate, matrix_rate, vector_rate)
    decays = (matrix_decay, matrix_decay, matrix_decay, matrix_decay, 0.0)
    results = [
        adam_update(
            masters[index],
            summed[index] * factor,
            firsts[index],
            seconds[index],
            rates[index],
            decays[index],
        )
        for index in range(5)
    ]
    momenta = tuple((item[0] for item in results))
    variances = tuple((item[1] for item in results))
    updated = tuple((item[2] for item in results))
    copies = tuple((item.astype(jnp.bfloat16) for item in updated))
    return (
        activations,
        input_grad,
        grad_norm.reshape(1),
        momenta[0],
        momenta[1],
        momenta[2],
        momenta[3],
        momenta[4],
        variances[0],
        variances[1],
        variances[2],
        variances[3],
        variances[4],
        updated[0],
        updated[1],
        updated[2],
        updated[3],
        updated[4],
        copies[0],
        copies[1],
        copies[2],
        copies[3],
        copies[4],
    )


def solution(mesh):
    return jax.shard_map(
        on_device,
        mesh=mesh,
        in_specs=(
            P(("dp", "fsdp"), None),
            P(("dp", "fsdp"), None),
            P(("dp", "fsdp"), None),
            P(("dp", "fsdp"), None),
            P(("dp", "fsdp"), None),
            P(("dp", "fsdp"), None),
            P(("dp", "fsdp"), None),
            P(None, ("dp", "fsdp")),
            P(("dp", "fsdp"), None),
            P(("dp", "fsdp"), None),
            P(("dp", "fsdp"), None),
            P(("dp", "fsdp"), None),
            P(None, ("dp", "fsdp")),
            P(("dp", "fsdp"), None),
            P(("dp", "fsdp"), None),
            P(("dp", "fsdp"), None),
            P(("dp", "fsdp"), None),
            P(None, ("dp", "fsdp")),
        ),
        out_specs=(
            P(("dp", "fsdp"), None),
            P(("dp", "fsdp"), None),
            P(),
            P(("dp", "fsdp"), None),
            P(("dp", "fsdp"), None),
            P(("dp", "fsdp"), None),
            P(("dp", "fsdp"), None),
            P(None, ("dp", "fsdp")),
            P(("dp", "fsdp"), None),
            P(("dp", "fsdp"), None),
            P(("dp", "fsdp"), None),
            P(("dp", "fsdp"), None),
            P(None, ("dp", "fsdp")),
            P(("dp", "fsdp"), None),
            P(("dp", "fsdp"), None),
            P(("dp", "fsdp"), None),
            P(("dp", "fsdp"), None),
            P(None, ("dp", "fsdp")),
            P(("dp", "fsdp"), None),
            P(("dp", "fsdp"), None),
            P(("dp", "fsdp"), None),
            P(("dp", "fsdp"), None),
            P(None, ("dp", "fsdp")),
        ),
        check_vma=False,
    )
```

profile of v0, /device:TPU:0, one launch (start us, length us, event | category | flops | bytes accessed | tf_op | source)
XLA Modules:
  0.0 1160.9 jit_solution(12365894638037846079)
XLA Ops:
  14.6 43.7 %all-gather = bf16[32,24,13]{1,2,0:T(8,128)(2,1)S(1)} all-gather(bf16[1,24,13]{1,2,0:T(8,128)(2,1)S(1)} %convert_bitcast_fusion.4), channel_id=1, replica_groups=mesh['dp'=4,'fsdp'=8] {'dp','fsdp'}, dimensions={0}, use_global_device_ids=true | all-gather | bytes 20592 | tf_op jit(solution)/shard_map/all_gather | solution.py:133
  60.8 13.2 %gather_fusion = bf16[2144,768]{1,0:T(8,128)(2,1)S(1)} fusion(bf16[4336,768]{1,0:T(8,128)(2,1)} %param.18, s32[3072]{0:T(1024)S(1)} %pad_clamp_fusion), kind=kCustom, calls=%fused_computation | custom fusion | bytes 6594944 | tf_op jit(solution)/shard_map/gather | solution.py:138
  78.4 13.1 %gather_fusion.1 = bf16[2144,768]{1,0:T(8,128)(2,1)} fusion(bf16[4336,768]{1,0:T(8,128)(2,1)} %param.20, s32[3072]{0:T(1024)S(1)} %pad_clamp_fusion), kind=kCustom, calls=%fused_computation.1 | custom fusion | bytes 6594944 | tf_op jit(solution)/shard_map/gather | solution.py:175
  91.5 11.2 fusion.6
  112.0 9.1 reshape.267
  133.9 9.5 reshape.269
  156.2 9.1 reshape.265
  283.2 72.8 %multiply_convert_fusion = (bf16[2144,3072]{1,0:T(8,128)(2,1)}, f32[2144,3072]{1,0:T(8,128)}, f32[2144,3072]{1,0:T(8,128)}) fusion(f32[3072]{0:T(1024)S(1)} %copy-done.63, bf16[768,3072]{1,0:T(8,128)(2,1)} %all-gather.10.cloned.1.call-done, f32[2144,768]{1,0:T(8,128)} %copy-done.7, f32[768]{0:T(1024)S(1)} %get-tuple-element.34, ...), kind=kOutput, calls=%fused_computation.8 | convolution fusion | flops 10559594496 | bytes 77204224 | tf_op jit(solution)/shard_map/dot_general | solution.py:158
  356.0 29.2 %convert_reduce_fusion = (f32[3072]{0:T(1024)}, bf16[2144,3072]{1,0:T(8,128)(2,1)}) fusion(f32[2144,3072]{1,0:T(8,128)} %get-tuple-element.66, bf16[3072,768]{1,0:T(8,128)(2,1)} %all-gather.12.cloned.1.call-done, bf16[2144,768]{1,0:T(8,128)(2,1)S(1)} %copy-done.22, f32[2144]{0:T(1024)S(1)} %copy-done.54, f32[2144,3072]{1,0:T(8,128)} %get-tuple-element.81, ...), kind=kOutput, calls=%fused_computation.6 | convolution fusion | flops 10233566208 | bytes 73908608 | tf_op jit(solution)/shard_map/dot_general | solution.py:45
  385.2 21.0 %multiply_reduce_fusion.2 = (f32[768]{0:T(1024)}, f32[2144]{0:T(1024)}, f32[768]{0:T(1024)}, f32[2144,768]{1,0:T(8,128)}) fusion(f32[2144,768]{1,0:T(8,128)} %copy-done.7, f32[2144]{0:T(1024)} %copy-done.50, f32[2144]{0:T(1024)S(1)} %broadcast_multiply_fusion, f32[768]{0:T(1024)S(1)} %get-tuple-element.35, bf16[2144,3072]{1,0:T(8,128)(2,1)} %get-tuple-element.90, ...), kind=kOutput, calls=%fused_computation.57 | convolution fusion | flops 10129829888 | bytes 31099008 | tf_op jit(solution)/shard_map/dot_general | solution.py:45
  414.9 23.9 %convert_reduce_fusion.4 = (f32[768]{0:T(1024)}, bf16[2144,768]{1,0:T(8,128)(2,1)}, f32[2144]{0:T(1024)}, f32[768]{0:T(1024)}, f32[2144,768]{1,0:T(8,128)}) fusion(f32[2144,768]{1,0:T(8,128)} %get-tuple-element.64, f32[2144]{0:T(1024)S(1)} %negate_multiply_fusion.2, f32[2144]{0:T(1024)} %convolution_reduce_fusion, bf16[2144,768]{1,0:T(8,128)(2,1)S(1)} %copy-done.22, ...), kind=kOutput, calls=%fused_computation.58 | convolution fusion | flops 10141356032 | bytes 44274816 | tf_op jit(solution)/shard_map/dot_general | solution.py:163
  468.7 14.3 %multiply_reduce_fusion = (f32[16,12,98]{2,1,0:T(8,128)S(1)}, f32[16,12,98,98]{2,3,1,0:T(8,128)}) fusion(f32[16,12,98,98]{2,3,1,0:T(8,128)} %copy-done, f32[16,12,98]{2,1,0:T(8,128)S(1)} %copy-done.23, bf16[16,98,12,64]{1,0,3,2:T(8,128)(2,1)} %reshape.266, bf16[16,98,12,64]{1,0,3,2:T(8,128)(2,1)} %reshape.277), kind=kOutput, calls=%fused_computation.26 | convolution fusion | flops 243384960 | bytes 19719168 | tf_op jit(solution)/shard_map/cqhe,ckhe->chqk/dot_general | solution.py:82
  642.2 15.7 %fusion.106 = f32[768,2304]{1,0:T(8,128)} fusion(bf16[2144,768]{1,0:T(8,128)(2,1)S(1)} %copy-done.2, f32[768]{0:T(1024)S(1)} %copy-done.69, f32[768]{0:T(1024)S(1)} %copy-done.57, f32[2144]{0:T(1024)S(1)} %copy-done.41, f32[2144]{0:T(1024)S(1)} %copy-done.39, bf16[2144,768]{1,0:T(8,128)(2,1)} %copy.150, bf16[2144,768]{1,0:T(8,128)(2,1)} %copy.149, ...), kind=kOutput, calls=%fused_computation.192 | convolution fusion | flops 7627014144 | bytes 20273920 | tf_op jit(solution)/shard_map/dot_general | solution.py:39
  658.7 19.8 %fusion.111 = f32[768,3072]{1,0:T(8,128)} fusion(bf16[2144,3072]{1,0:T(8,128)(2,1)} %get-tuple-element.90, f32[2144,768]{1,0:T(8,128)} %copy-done.7, f32[768]{0:T(1024)S(1)} %copy-done.67, f32[768]{0:T(1024)S(1)} %copy-done.61, f32[2144]{0:T(1024)S(1)} %copy-done.51, f32[2144]{0:T(1024)S(1)} %copy-done.43), kind=kOutput, calls=%fused_computation.195 | convolution fusion | flops 10124894208 | bytes 29219584 | tf_op jit(solution)/shard_map/dot_general | solution.py:39
  679.2 17.9 %fusion.103 = f32[3072,768]{1,0:T(8,128)} fusion(bf16[2144,3072]{1,0:T(8,128)(2,1)} %get-tuple-element.65, bf16[2144,768]{1,0:T(8,128)(2,1)} %gather_fusion.1, f32[2144]{0:T(1024)S(1)} %copy-done.55), kind=kOutput, calls=%fused_computation.191 | convolution fusion | flops 10121601024 | bytes 25911680 | tf_op jit(solution)/shard_map/dot_general | solution.py:39
  697.1 9.0 convert_element_type.130
  706.2 9.1 convert_element_type.114
  721.7 15.5 %fusion.113 = (f32[768]{0:T(1024)S(1)}, f32[2144]{0:T(1024)S(1)}, f32[2144,768]{1,0:T(8,128)}) fusion(f32[768]{0:T(1024)S(1)} %copy-done.57, f32[2144]{0:T(1024)S(1)} %copy-done.39, bf16[2144,768]{1,0:T(8,128)(2,1)S(1)} %copy-done.2, bf16[768,2304]{1,0:T(8,128)(2,1)} %all-gather.6.cloned.1.call-done, bf16[2144,768]{1,0:T(8,128)(2,1)} %copy.150, ...), kind=kOutput, calls=%fused_computation.197 | convolution fusion | flops 7627011072 | bytes 23321344 | tf_op jit(solution)/shard_map/dot_general | solution.py:45
  743.1 32.7 %scatter_custom_fusion.1 = f32[4336,768]{1,0:T(8,128)} fusion(f32[4336,768]{1,0:T(8,128)} %convert_element_type.130, s32[2144]{0:T(1024)} %copy-done.53, f32[2144,768]{1,0:T(8,128)} %get-tuple-element.64, f32[768]{0:T(1024)S(1)} %copy-done.59, f32[2144]{0:T(1024)S(1)} %copy-done.52, f32[2144]{0:T(1024)S(1)} %negate_multiply_fusion.1, ...), kind=kCustom, calls=%fused_computation.59 | custom fusion | flops 21405696 | bytes 29843712 | tf_op jit(solution)/shard_map/scatter-add | solution.py:204
  784.4 32.8 %scatter_custom_fusion = f32[4336,768]{1,0:T(8,128)} fusion(f32[4336,768]{1,0:T(8,128)} %convert_element_type.114, s32[2144]{0:T(1024)} %copy-done.53, f32[2144,768]{1,0:T(8,128)} %get-tuple-element.83, f32[2144]{0:T(1024)S(1)} %copy-done.55), kind=kCustom, calls=%fused_computation.65 | custom fusion | flops 3293184 | bytes 19915136 | tf_op jit(solution)/shard_map/scatter-add | solution.py:166
  818.7 37.3 %all-reduce = f32[13,768]{1,0:T(8,128)S(1)} all-reduce(f32[13,768]{1,0:T(8,128)S(1)} %concatenate.32), channel_id=6, replica_groups=mesh['dp'=4,'fsdp'=8] {'dp','fsdp'}, use_global_device_ids=true, to_apply=%region_33.0.clone | all-reduce | flops 9984 | bytes 79872
  861.1 92.3 %reduce-scatter.10.cloned.1.call-done = f32[24,3072]{1,0:T(8,128)} async-done(((f32[768,3072]{1,0:T(8,128)}), f32[24,3072]{1,0:T(8,128)}) %reduce-scatter.10.cloned.1.call-update) | async-done | bytes 294928 | tf_op jit(solution)/shard_map/reduce_scatter | solution.py:228
  955.8 139.2 %reduce-scatter.12.cloned.1.call-done = f32[96,768]{1,0:T(8,128)} async-done(((f32[3072,768]{1,0:T(8,128)}), f32[96,768]{1,0:T(8,128)}) %reduce-scatter.12.cloned.1.call-update) | async-done | bytes 294928 | tf_op jit(solution)/shard_map/reduce_scatter | solution.py:229
  1106.5 39.9 %psum.7 = f32[]{:T(128)} all-reduce(f32[]{:T(128)S(6)} %add.268), channel_id=1, replica_groups=mesh['dp'=4,'fsdp'=8] {'dp','fsdp'}, use_global_device_ids=true, to_apply=%region_35.0 | all-reduce | flops 1 | bytes 8 | tf_op jit(solution)/shard_map/psum | solution.py:235
  (325 shorter events, 409.0 us)
Async XLA Ops:
  7.2 84.3 %all-gather.6.cloned.1.call-start = ((), (), s32[]{:S(2)}) async-start(), calls=%async_computation.4 | async-start | bytes 3649536 | tf_op jit(solution)/shard_map/all_gather | solution.py:129
  8.9 261.5 %all-gather.8.cloned.1.call-start = ((), (), s32[]{:S(2)}) async-start(), calls=%async_computation.5 | async-start | bytes 1216512 | tf_op jit(solution)/shard_map/all_gather | solution.py:130
  10.4 272.7 %all-gather.10.cloned.1.call-start = ((), (), s32[]{:S(2)}) async-start(), calls=%async_computation.6 | async-start | bytes 4866048 | tf_op jit(solution)/shard_map/all_gather | solution.py:131
  12.2 343.8 %all-gather.12.cloned.1.call-start = ((), (), s32[]{:S(2)}) async-start(), calls=%async_computation.7 | async-start | bytes 4866048 | tf_op jit(solution)/shard_map/all_gather | solution.py:132
  13.9 842.8 %reduce-scatter.8.cloned.1.call-start = ((), (), s32[]{:S(2)}) async-start(), calls=%async_computation.9 | async-start | bytes 2433024 | tf_op jit(solution)/shard_map/reduce_scatter | solution.py:227
  59.2 211.2 %copy-start.71 = (f32[768]{0:T(1024)}, f32[768]{0:T(1024)S(1)}, u32[]{:S(2)}) copy-start(f32[768]{0:T(1024)S(1)} %get-tuple-element.36) | copy-start | bytes 9220
  59.2 223.9 %copy-start.66 = (f32[768]{0:T(1024)}, f32[768]{0:T(1024)S(1)}, u32[]{:S(2)}) copy-start(f32[768]{0:T(1024)S(1)} %get-tuple-element.34) | copy-start | bytes 9220
  59.2 347.8 %copy-start.60 = (f32[768]{0:T(1024)}, f32[768]{0:T(1024)S(1)}, u32[]{:S(2)}) copy-start(f32[768]{0:T(1024)S(1)} %get-tuple-element.35) | copy-start | bytes 9220
  73.9 196.5 %copy-start.1 = (bf16[2144,768]{1,0:T(8,128)(2,1)}, bf16[2144,768]{1,0:T(8,128)(2,1)S(1)}, u32[]{:S(2)}) copy-start(bf16[2144,768]{1,0:T(8,128)(2,1)S(1)} %gather_fusion) | copy-start | bytes 9879556
  278.8 128.2 %copy-start.42 = (f32[2144]{0:T(1024)}, f32[2144]{0:T(1024)S(1)}, u32[]{:S(2)}) copy-start(f32[2144]{0:T(1024)S(1)} %broadcast_multiply_fusion) | copy-start | bytes 25732
  283.1 72.9 %copy-start.50 = (f32[2144]{0:T(1024)}, f32[2144]{0:T(1024)S(1)}, u32[]{:S(2)}) copy-start(f32[2144]{0:T(1024)S(1)} %fusion.96) | copy-start | bytes 25732
  283.1 72.9 %copy-start.22 = (bf16[2144,768]{1,0:T(8,128)(2,1)S(1)}, bf16[2144,768]{1,0:T(8,128)(2,1)}, u32[]{:S(2)}) copy-start(bf16[2144,768]{1,0:T(8,128)(2,1)} %gather_fusion.1) | copy-start | bytes 9879556
  283.2 72.8 %copy-start.54 = (f32[2144]{0:T(1024)S(1)}, f32[2144]{0:T(1024)}, u32[]{:S(2)}) copy-start(f32[2144]{0:T(1024)} %convolution_reduce_fusion) | copy-start | bytes 25732
  592.4 265.8 %reduce-scatter.6.cloned.1.call-start = ((), (), s32[]{:S(2)}) async-start(), calls=%async_computation.8 | async-start | bytes 7299072 | tf_op jit(solution)/shard_map/reduce_scatter | solution.py:226
  658.0 295.5 %reduce-scatter.10.cloned.1.call-start = ((), (), s32[]{:S(2)}) async-start(), calls=%async_computation.10 | async-start | bytes 9732096 | tf_op jit(solution)/shard_map/reduce_scatter | solution.py:228
  678.5 416.5 %reduce-scatter.12.cloned.1.call-start = ((), (), s32[]{:S(2)}) async-start(), calls=%async_computation.11 | async-start | bytes 9732096 | tf_op jit(solution)/shard_map/reduce_scatter | solution.py:229
  1098.0 51.0 %copy-start.25 = (f32[24,3072]{1,0:T(8,128)S(1)}, f32[24,3072]{1,0:T(8,128)}, u32[]{:S(2)}) copy-start(f32[24,3072]{1,0:T(8,128)} %param.23) | copy-start | bytes 884740
  1098.0 52.1 %copy-start.34 = (f32[24,768]{1,0:T(8,128)S(1)}, f32[24,768]{1,0:T(8,128)}, u32[]{:S(2)}) copy-start(f32[24,768]{1,0:T(8,128)} %param.22) | copy-start | bytes 221188
  1098.0 52.1 %copy-start.35 = (f32[24,768]{1,0:T(8,128)S(1)}, f32[24,768]{1,0:T(8,128)}, u32[]{:S(2)}) copy-start(f32[24,768]{1,0:T(8,128)} %reduce-scatter.8.cloned.1.call-done) | copy-start | bytes 221188
  1098.1 52.1 %copy-start.47 = (f32[24,768]{1,0:T(8,128)S(1)}, f32[24,768]{1,0:T(8,128)}, u32[]{:S(2)}) copy-start(f32[24,768]{1,0:T(8,128)} %param.32) | copy-start | bytes 221188
  1098.1 53.7 %copy-start.28 = (f32[24,2304]{1,0:T(8,128)S(1)}, f32[24,2304]{1,0:T(8,128)}, u32[]{:S(2)}) copy-start(f32[24,2304]{1,0:T(8,128)} %reduce-scatter.6.cloned.1.call-done) | copy-start | bytes 663556
  1098.1 53.7 %copy-start.29 = (f32[24,2304]{1,0:T(8,128)S(1)}, f32[24,2304]{1,0:T(8,128)}, u32[]{:S(2)}) copy-start(f32[24,2304]{1,0:T(8,128)} %param.21) | copy-start | bytes 663556
  1098.1 53.7 %copy-start.36 = (f32[24,2304]{1,0:T(8,128)S(1)}, f32[24,2304]{1,0:T(8,128)}, u32[]{:S(2)}) copy-start(f32[24,2304]{1,0:T(8,128)} %param.31) | copy-start | bytes 663556
  1098.1 53.7 %copy-start.37 = (f32[24,2304]{1,0:T(8,128)S(1)}, f32[24,2304]{1,0:T(8,128)}, u32[]{:S(2)}) copy-start(f32[24,2304]{1,0:T(8,128)} %param.26) | copy-start | bytes 663556
  (67 other events, 1023.4 us)
Sparse Core Ops, SparseCore 0:
  11.5 62.8 all-gather.5
  77.8 52.8 all-gather.7
  134.2 62.5 all-gather.9
  200.1 62.4 all-gather.11
  592.6 95.5 reduce-scatter.7
  694.6 118.2 reduce-scatter.5
  818.8 134.6 reduce-scatter.9
  960.4 134.5 reduce-scatter.11
where the time goes:
time: 1180 us; the launch traced here: 1160 us
  matrix products  312 us (26%)
  local copies, waits for them, and re-layouts  296 us (25%)
  waiting for transfers between devices  232 us (20%)
  other arithmetic  179 us (15%)
  blocking collectives  121 us (10%)
  between operations  20.7 us (2%)
    reduce_scatter x1, waiting for transfers between devices, on_device(): lax.psum_scatter(grad_contract, ('dp', 'fsdp'), scatter_dimension=0, tile...  139 us
    reduce_scatter x1, waiting for transfers between devices, on_device(): lax.psum_scatter(grad_expand, ('dp', 'fsdp'), scatter_dimension=0, tiled=...  92.3 us
    dot_general x1, matrix products, on_device(): jnp.dot(normed_two_low, full[2], preferred_element_type=jnp.float32)  72.8 us
    dot_general x4, matrix products, inner(): lax.dot_general(left, right, (((1,), (1,)), ((), ())), preferred_element_...  72.1 us
    dot_general x4, matrix products, outer(): lax.dot_general(left, right, (((0,), (0,)), ((), ())), preferred_element_...  57.8 us
    all_gather x1, blocking collectives, on_device(): lax.all_gather(vectors.astype(jnp.bfloat16), ('dp', 'fsdp'), axis=1, tile...  43.7 us
    psum x1, blocking collectives, on_device(): total_squares = lax.psum(local_squares, ('dp', 'fsdp'))  39.9 us
    reshape x6, local copies, waits for them, and re-layouts, from_crops(): return joined.reshape(count * KEEP, D)  37.6 us
  transfers between devices with their start and end apart: 8, of which 2 were waited for; matrix products, arithmetic and copies ran while one was open for 45% of the time, Pallas kernels for 0%

commit v1 on v0

v1 whole, which is shorter than its diff:
```python
import functools
import math

import jax
import jax.numpy as jnp
from jax import lax
from jax.experimental import pallas as pl
from jax.experimental.pallas import tpu as pltpu
from jax.sharding import PartitionSpec as P

D = 768
HEADS = 12
HEAD_DIM = 64
KEEP_GLOBAL = 98
KEEP_LOCAL = 18
KEEP = 268
PARAMS = 7087872
STEP = 5

norm_eps = 1e-06
clip_share = 0.05
matrix_rate = 0.04
vector_rate = 0.3
matrix_decay = 0.05
first_beta = 0.5
second_beta = 0.5
adam_eps = 1e-08

AXES = ("dp", "fsdp")
BF = jnp.bfloat16
F32 = jnp.float32
NT = (((1,), (1,)), ((), ()))
TN = (((0,), (0,)), ((), ()))
PAD = -(-KEEP // 16) * 16
PAIRS = HEADS // 2
PW = 2 * HEAD_DIM
GROUPS = 3
CHUNKS = 2
HIDDEN = 4 * D
HALF = HIDDEN // CHUNKS // 2
VMEM_LIMIT = 60 * 2**20
NEG = -1e30
SEGMENTS = (
    (0, 112, 0, KEEP_GLOBAL),
    (96, 112, KEEP_GLOBAL, 2 * KEEP_GLOBAL),
    (192, 80, 2 * KEEP_GLOBAL, KEEP),
)


def nn(left, right):
    return jnp.dot(left, right, preferred_element_type=F32)


def nt(left, right):
    return lax.dot_general(left, right, NT, preferred_element_type=F32)


def tn(left, right):
    return lax.dot_general(left, right, TN, preferred_element_type=F32)


def params(**more):
    return pltpu.CompilerParams(vmem_limit_bytes=VMEM_LIMIT, **more)


def cost(flops, moved, exps=0):
    return pl.CostEstimate(flops=int(flops), bytes_accessed=int(moved), transcendentals=int(exps))


def whole(shape):
    return pl.BlockSpec(shape, lambda *_: (0,) * len(shape))


ANY = pl.BlockSpec(memory_space=pl.ANY)
SMEM = pl.BlockSpec(memory_space=pltpu.SMEM)


def normalize(values):
    centred = values - jnp.mean(values, axis=-1, keepdims=True)
    spread = jnp.mean(centred * centred, axis=-1, keepdims=True)
    inverse = lax.rsqrt(spread + norm_eps)
    return centred * inverse, inverse


def norm_back(grad, normed, inverse, gain):
    pulled = grad * gain
    return inverse * (
        pulled
        - jnp.mean(pulled, axis=-1, keepdims=True)
        - normed * jnp.mean(pulled * normed, axis=-1, keepdims=True)
    )


def column_sum(values):
    return jnp.sum(values, axis=0, keepdims=True)


def window_start(image, image_tokens, rows, window):
    return jnp.minimum((image_tokens * image) // 16, (rows - window) // 16) * 16


def pick_kernel(image_tokens, rows, window, slots, vec, tokens, cot, picked, grads, normed, mlp):
    image = pl.program_id(0)
    shift = image_tokens * image - window_start(image, image_tokens, rows, window)
    place = slots[0] + shift
    hot = (lax.broadcasted_iota(jnp.int32, (PAD, window), 1) == place).astype(F32).astype(BF)
    values = nn(hot, tokens[...])
    grad_rows = nn(hot, cot[...])
    picked[...] = values.astype(BF)
    grads[...] = grad_rows.astype(BF)
    gain = vec[0:1, :].astype(F32)
    shift_one = vec[1:2, :].astype(F32)
    router = vec[8:9, :].astype(F32)
    unit, _ = normalize(values)
    normed[...] = (unit * gain + shift_one).astype(BF)
    routed = jnp.sum(values * router, axis=-1, keepdims=True)
    mlp[...] = (routed * grad_rows).astype(BF)


def pick(tokens, cot, slots, vec):
    rows = tokens.shape[0]
    count = slots.shape[0]
    image_tokens = rows // count
    window = -(-(image_tokens + 15) // 16) * 16
    start = functools.partial(
        window_start, image_tokens=image_tokens, rows=rows, window=window
    )
    source = pl.BlockSpec((pl.Element(window), pl.Element(D)), lambda i: (start(i), 0))
    block = pl.BlockSpec((PAD, D), lambda i: (i, 0))
    shape = jax.ShapeDtypeStruct((count * PAD, D), BF)
    return pl.pallas_call(
        functools.partial(pick_kernel, image_tokens, rows, window),
        grid=(count,),
        in_specs=[
            pl.BlockSpec((1, PAD, 1), lambda i: (i, 0, 0)),
            whole((16, D)),
            source,
            source,
        ],
        out_specs=(block,) * 4,
        out_shape=(shape,) * 4,
        compiler_params=params(),
        cost_estimate=cost(4 * count * PAD * window * D, 4 * rows * D + 8 * count * PAD * D),
        name="pick_rows",
    )(slots, vec, tokens, cot)


def local_mask():
    first, rows, low, high = SEGMENTS[2]
    slot = jnp.arange(rows) + first
    crop = jnp.where((slot >= low) & (slot < high), (slot - low) // KEEP_LOCAL, -1)
    same = (crop[:, None] == crop[None, :]) & (crop[:, None] >= 0)
    bias = jnp.where(same, 0.0, NEG).astype(F32)
    return jnp.concatenate([bias, bias], axis=1)


def lanes_of(rows):
    return lax.broadcasted_iota(jnp.int32, (rows, PW), 1) < HEAD_DIM


def split_heads(values):
    first = lanes_of(values.shape[0])
    zero = jnp.zeros_like(values)
    return jnp.concatenate(
        [jnp.where(first, values, zero), jnp.where(first, zero, values)], axis=0
    )


def join_heads(values):
    rows = values.shape[0] // 2
    return jnp.where(lanes_of(rows), values[:rows], values[rows:])


def probabilities(segment, mask, keys, queries):
    first, rows, low, high = segment
    scores = nt(keys, queries)
    if low == 2 * KEEP_GLOBAL:
        scores = scores + mask
    else:
        slot = lax.broadcasted_iota(jnp.int32, (rows, 1), 0) + first
        scores = jnp.where((slot >= low) & (slot < high), scores, NEG)
    grown = jnp.exp(scores - jnp.max(scores, axis=0, keepdims=True))
    return grown * (1.0 / jnp.sum(grown, axis=0, keepdims=True))


def attention(query, key_rows, value, mask, store):
    parts = []
    for segment in SEGMENTS:
        rows = slice(segment[0], segment[0] + segment[1])
        halves = split_heads(query[rows] * BF(HEAD_DIM**-0.5))
        probs = probabilities(segment, mask, key_rows[rows], halves).astype(BF)
        parts.append(join_heads(tn(probs, value[rows])))
    one, two, three = parts
    slot = lax.broadcasted_iota(jnp.int32, (16, 1), 0)
    store(0, one[:96])
    store(96, jnp.where(slot + 96 < KEEP_GLOBAL, one[96:], two[:16]))
    store(112, two[16:96])
    store(192, jnp.where(slot + 192 < 2 * KEEP_GLOBAL, two[96:], three[:16]))
    store(208, three[16:])


def attention_back(query, key_rows, value, grad, mask):
    results = []
    for segment in SEGMENTS:
        first, count, low, high = segment
        rows = slice(first, first + count)
        halves = split_heads(query[rows] * BF(HEAD_DIM**-0.5))
        slot = lax.broadcasted_iota(jnp.int32, (count, 1), 0) + first
        kept = jnp.where((slot >= low) & (slot < high), grad[rows], jnp.zeros((), BF))
        grads = split_heads(kept)
        probs = probabilities(segment, mask, key_rows[rows], halves)
        grad_probs = nt(value[rows], grads)
        weighted = jnp.sum(probs * grad_probs, axis=0, keepdims=True)
        grad_scores = (probs * (grad_probs - weighted)).astype(BF)
        grad_value = nn(probs.astype(BF), grads)
        grad_key = nn(grad_scores, halves)
        grad_query = join_heads(tn(grad_scores, key_rows[rows])) * HEAD_DIM**-0.5
        results.append((grad_query, grad_key, grad_value))
    joined = []
    for one, two, three in zip(*results):
        joined.append(
            jnp.concatenate(
                [
                    one[:96],
                    one[96:] + two[:16],
                    two[16:96],
                    two[96:] + three[:16],
                    three[16:],
                ],
                axis=0,
            )
        )
    return joined


def pair_lanes(place, group, own):
    core = place[2]
    pair = 2 * group + (core if own else 1 - core)
    return pl.ds(pl.multiple_of(pair * PW, PW), PW)


def heads_kernel(group, place, mask, vec, normed, own_w, other_w, *outs):
    rows = normed[...]
    for own, weight, mixed, heads in (
        (True, own_w, outs[0], outs[2]),
        (False, other_w, outs[1], outs[3]),
    ):
        lanes = pair_lanes(place, group, own)
        product = nn(rows, weight[...])
        query = (product[:, :PW] + vec[2:3, lanes].astype(F32)).astype(BF)
        key_rows = product[:, PW : 2 * PW].astype(BF)
        value = (product[:, 2 * PW :] + vec[3:4, lanes].astype(F32)).astype(BF)
        mixed[:, :PW] = query
        mixed[:, PW : 2 * PW] = key_rows
        mixed[:, 2 * PW :] = value

        def store(first, values, heads=heads):
            heads[first : first + values.shape[0], :] = values.astype(BF)

        attention(query, key_rows, value, mask[...], store)


def heads_forward(group, place, mask, vec, normed, own_w, other_w):
    rows = normed.shape[0]
    count = rows // PAD
    block = pl.BlockSpec((PAD, 3 * PW), lambda i: (i, 0))
    small = pl.BlockSpec((PAD, PW), lambda i: (i, 0))
    return pl.pallas_call(
        functools.partial(heads_kernel, group),
        grid=(count,),
        in_specs=[
            SMEM,
            whole(mask.shape),
            whole((16, D)),
            pl.BlockSpec((PAD, D), lambda i: (i, 0)),
            whole((D, 3 * PW)),
            whole((D, 3 * PW)),
        ],
        out_specs=(block, block, small, small),
        out_shape=(jax.ShapeDtypeStruct((rows, 3 * PW), BF),) * 2
        + (jax.ShapeDtypeStruct((rows, PW), BF),) * 2,
        compiler_params=params(),
        cost_estimate=cost(6 * 2 * rows * D * PW + rows * 2e5, 8 * rows * D, rows * 400),
        name=f"attention_{group}",
    )(place, mask, vec, normed, own_w, other_w)


def heads_back_kernel(
    group, count, place, mask, grad_attended, normed, w_out, mixed_own, mixed_other, *rest
):
    (gm_own, gm_other, gw_own, gw_other, sums_own, sums_other, kept_normed, kept_own, kept_other) = rest
    step = pl.program_id(0)

    @pl.when(step == 0)
    def _():
        sums_own[...] = jnp.zeros_like(sums_own)
        sums_other[...] = jnp.zeros_like(sums_other)

    @pl.when(step < count)
    def _():
        rows = pl.ds(pl.multiple_of(step * PAD, 16), PAD)
        kept_normed[rows, :] = normed[...]
        incoming = grad_attended[...]
        for own, mixed, out, kept, sums in (
            (False, mixed_other, gm_other, kept_other, sums_other),
            (True, mixed_own, gm_own, kept_own, sums_own),
        ):
            lanes = pair_lanes(place, group, own)
            grad_heads = nt(incoming, w_out[lanes, :]).astype(BF)
            parts = attention_back(
                mixed[:, :PW], mixed[:, PW : 2 * PW], mixed[:, 2 * PW :], grad_heads, mask[...]
            )
            for index, part in enumerate(parts):
                low = part.astype(BF)
                columns = slice(index * PW, (index + 1) * PW)
                out[:, columns] = low
                kept[rows, columns] = low
                sums[0:1, columns] += column_sum(low.astype(F32))

    @pl.when(step == count)
    def _():
        gw_other[...] = tn(kept_normed[...], kept_other[...]).astype(BF)
        gw_own[...] = tn(kept_normed[...], kept_own[...]).astype(BF)


def heads_backward(group, place, mask, grad_attended, normed, w_out, mixed_own, mixed_other):
    rows = normed.shape[0]
    count = rows // PAD
    last = count - 1
    wide = pl.BlockSpec((PAD, D), lambda i: (jnp.minimum(i, last), 0))
    block = pl.BlockSpec((PAD, 3 * PW), lambda i: (jnp.minimum(i, last), 0))
    mixed_shape = jax.ShapeDtypeStruct((rows, 3 * PW), BF)
    weight_shape = jax.ShapeDtypeStruct((D, 3 * PW), BF)
    sum_shape = jax.ShapeDtypeStruct((8, 3 * PW), F32)
    return pl.pallas_call(
        functools.partial(heads_back_kernel, group, count),
        grid=(count + 1,),
        in_specs=[SMEM, whole(mask.shape), wide, wide, whole((D, D)), block, block],
        out_specs=(block, block)
        + (whole((D, 3 * PW)),) * 2
        + (whole((8, 3 * PW)),) * 2,
        out_shape=(mixed_shape,) * 2 + (weight_shape,) * 2 + (sum_shape,) * 2,
        scratch_shapes=[
            pltpu.VMEM((rows, D), BF),
            pltpu.VMEM((rows, 3 * PW), BF),
            pltpu.VMEM((rows, 3 * PW), BF),
        ],
        compiler_params=params(),
        cost_estimate=cost(
            2 * rows * D * 2 * PW + 2 * rows * D * 6 * PW + rows * 5e5, 12 * rows * D, rows * 400
        ),
        name=f"attention_back_{group}",
    )(place, mask, grad_attended, normed, w_out, mixed_own, mixed_other)


def mix_kernel(place, vec, picked, own_w, other_w, *refs):
    heads = refs[: 2 * GROUPS]
    attended, normed, joined, w_full = refs[2 * GROUPS :]
    core = place[2]
    half = D // 2

    @pl.when(pl.program_id(0) == 0)
    def _():
        w_full[:, pl.ds(pl.multiple_of(core * half, 128), half)] = own_w[...]
        w_full[:, pl.ds(pl.multiple_of((1 - core) * half, 128), half)] = other_w[...]

    for group in range(GROUPS):
        joined[:, pair_lanes(place, group, True)] = heads[2 * group][...]
        joined[:, pair_lanes(place, group, False)] = heads[2 * group + 1][...]
    result = nn(joined[...], w_full[...]) + vec[4:5, :].astype(F32)
    attended[...] = result
    unit, _ = normalize(picked[...].astype(F32) + result)
    normed[...] = (unit * vec[5:6, :].astype(F32) + vec[6:7, :].astype(F32)).astype(BF)


def mix(place, vec, picked, own_w, other_w, heads):
    rows = picked.shape[0]
    size = 2 * PAD
    wide = pl.BlockSpec((size, D), lambda i: (i, 0))
    small = pl.BlockSpec((size, PW), lambda i: (i, 0))
    return pl.pallas_call(
        mix_kernel,
        grid=(rows // size,),
        in_specs=[SMEM, whole((16, D)), wide, whole((D, D // 2)), whole((D, D // 2))]
        + [small] * (2 * GROUPS),
        out_specs=(wide, wide, wide, whole((D, D))),
        out_shape=(
            jax.ShapeDtypeStruct((rows, D), F32),
            jax.ShapeDtypeStruct((rows, D), BF),
            jax.ShapeDtypeStruct((rows, D), BF),
            jax.ShapeDtypeStruct((D, D), BF),
        ),
        compiler_params=params(),
        cost_estimate=cost(2 * rows * D * D, 12 * rows * D),
        name="project_and_norm",
    )(place, vec, picked, own_w, other_w, *heads)


ERF_P = 0.3275911 / math.sqrt(2.0)
ERF_A = (0.254829592, -0.284496736, 1.421413741, -1.453152027, 1.061405429)


def gelu_and_slope(values):
    t = 1.0 / (1.0 + ERF_P * jnp.abs(values))
    bell = jnp.exp(-0.5 * values * values)
    tail = (0.5 * ERF_A[4]) * t + 0.5 * ERF_A[3]
    for factor in (ERF_A[2], ERF_A[1], ERF_A[0]):
        tail = tail * t + 0.5 * factor
    tail = tail * t * bell
    below = jnp.where(values >= 0, 1.0 - tail, tail)
    return values * below, below + values * bell * (1.0 / math.sqrt(2.0 * math.pi))


TILE = 256


def mlp_kernel(chunk, steps, size, place, bias, normed, grad, *refs):
    weights = refs[:4]
    refs = refs[4:]
    if chunk:
        out_before, back_before = refs[:2]
        refs = refs[2:]
    (out, back, gw1_other, gw2_other, gw1_own, gw2_own, sums) = refs[:7]
    kept_normed, kept_grad, kept_active, kept_before = refs[7:]
    step = pl.program_id(0)
    core = place[2]
    tiles = HALF // TILE

    @pl.when(step == 0)
    def _():
        sums[...] = jnp.zeros_like(sums)

    @pl.when(step < steps)
    def _():
        rows = pl.ds(pl.multiple_of(step * size, 16), size)
        left = normed[...]
        right = grad[...]
        kept_normed[rows, :] = left
        kept_grad[rows, :] = right
        for half in range(2):
            parity = core if half else 1 - core
            up, down = weights[2 * half], weights[2 * half + 1]
            for tile in range(tiles):
                columns = slice(tile * TILE, (tile + 1) * TILE)
                kept = slice(half * HALF + tile * TILE, half * HALF + (tile + 1) * TILE)
                before = nn(left, up[:, columns]) + bias[2 * chunk + parity, :, columns]
                active, slope = gelu_and_slope(before)
                kept_active[rows, kept] = active.astype(BF)
                low = (nt(right, down[columns, :]) * slope).astype(BF)
                kept_before[rows, kept] = low
                sums[parity, :, columns] += column_sum(low.astype(F32))
        result = nn(kept_active[rows, :HALF], weights[1][...])
        result += nn(kept_active[rows, HALF:], weights[3][...])
        pulled = nt(kept_before[rows, :HALF], weights[0][...])
        pulled += nt(kept_before[rows, HALF:], weights[2][...])
        if chunk:
            result += out_before[...]
            pulled += back_before[...]
        out[...] = result
        back[...] = pulled

    @pl.when(step >= steps)
    def _():
        tile = step - steps
        columns = pl.ds(pl.multiple_of(tile * TILE, TILE), TILE)
        for_up = tn(kept_normed[...], kept_before[:, columns]).astype(BF)
        for_down = tn(kept_active[:, columns], kept_grad[...]).astype(BF)

        @pl.when(tile < tiles)
        def _():
            gw1_other[...] = for_up
            gw2_other[...] = for_down

        @pl.when(tile >= tiles)
        def _():
            gw1_own[...] = for_up
            gw2_own[...] = for_down


def mlp(chunk, place, bias, normed, grad, weights, sums_before):
    rows = normed.shape[0]
    size = 2 * PAD
    steps = rows // size
    last = steps - 1
    tiles = HALF // TILE
    wide = pl.BlockSpec((size, D), lambda i: (jnp.minimum(i, last), 0))
    once = dict(pipeline_mode=pl.Buffered(1))
    up = pl.BlockSpec((D, HALF), lambda i: (0, 0), **once)
    down = pl.BlockSpec((HALF, D), lambda i: (0, 0), **once)

    def tile_of(i, first):
        return jnp.clip(i - steps - first, 0, tiles - 1)

    def gw1(first):
        return pl.BlockSpec((D, TILE), lambda i: (0, tile_of(i, first)))

    def gw2(first):
        return pl.BlockSpec((TILE, D), lambda i: (tile_of(i, first), 0))

    total = jax.ShapeDtypeStruct((rows, D), F32)
    up_shape = jax.ShapeDtypeStruct((D, HALF), BF)
    down_shape = jax.ShapeDtypeStruct((HALF, D), BF)
    return pl.pallas_call(
        functools.partial(mlp_kernel, chunk, steps, size),
        grid=(steps + 2 * tiles,),
        in_specs=[SMEM, whole(bias.shape), wide, wide, up, down, up, down]
        + [wide] * len(sums_before),
        out_specs=(wide, wide, gw1(0), gw2(0), gw1(tiles), gw2(tiles), whole((2, 1, HALF))),
        out_shape=(
            total,
            total,
            up_shape,
            down_shape,
            up_shape,
            down_shape,
            jax.ShapeDtypeStruct((2, 1, HALF), F32),
        ),
        scratch_shapes=[
            pltpu.VMEM((rows, D), BF),
            pltpu.VMEM((rows, D), BF),
            pltpu.VMEM((rows, 2 * HALF), BF),
            pltpu.VMEM((rows, 2 * HALF), BF),
        ],
        compiler_params=params(),
        cost_estimate=cost(
            24 * rows * D * HALF, 12 * rows * D + 16 * D * HALF, 4 * rows * HALF
        ),
        name=f"feed_forward_{chunk}",
    )(place, bias, normed, grad, *weights, *sums_before)


def turn_kernel(steps, size, place, vec, picked, grads, attended, out, back, heads, *refs):
    (grad_attended, carry, values, sums, gw_own, gw_other, kept_heads, kept_grad) = refs
    step = pl.program_id(0)
    core = place[2]
    half = D // 2

    @pl.when(step == 0)
    def _():
        sums[...] = jnp.zeros_like(sums)

    @pl.when(step < steps)
    def _():
        rows = pl.ds(pl.multiple_of(step * size, 16), size)
        inputs = picked[...].astype(F32)
        grad_rows = grads[...].astype(F32)
        router = vec[8:9, :].astype(F32)
        routed = jnp.sum(inputs * router, axis=-1, keepdims=True)
        mixed = attended[...]
        branch = mixed + out[...] + vec[7:8, :].astype(F32)
        values[...] = (inputs + routed * branch).astype(BF)
        grad_routed = jnp.sum(grad_rows * branch, axis=-1, keepdims=True)
        grad_branch = routed * grad_rows
        unit, inverse = normalize(inputs + mixed)
        pulled = back[...]
        residual = norm_back(pulled, unit, inverse, vec[5:6, :].astype(F32))
        low = (grad_branch + residual).astype(BF)
        grad_attended[...] = low
        kept_grad[rows, :] = low
        kept_heads[rows, :] = heads[...]
        carry[...] = residual + grad_routed * router
        sums[0:1, :] += column_sum(low.astype(F32))
        sums[1:2, :] += column_sum(pulled * unit)
        sums[2:3, :] += column_sum(pulled)
        sums[3:4, :] += column_sum(grad_branch.astype(BF).astype(F32))
        sums[4:5, :] += column_sum(inputs * grad_routed)

    @pl.when(step == steps)
    def _():
        own = pl.ds(pl.multiple_of(core * half, 128), half)
        other = pl.ds(pl.multiple_of((1 - core) * half, 128), half)
        gw_own[...] = tn(kept_heads[...], kept_grad[:, own]).astype(BF)
        gw_other[...] = tn(kept_heads[...], kept_grad[:, other]).astype(BF)


def turn(place, vec, picked, grads, attended, out, back, heads):
    rows = picked.shape[0]
    size = 2 * PAD
    steps = rows // size
    last = steps - 1
    wide = pl.BlockSpec((size, D), lambda i: (jnp.minimum(i, last), 0))
    return pl.pallas_call(
        functools.partial(turn_kernel, steps, size),
        grid=(steps + 1,),
        in_specs=[SMEM, whole((16, D))] + [wide] * 6,
        out_specs=(wide, wide, wide, whole((8, D)), whole((D, D // 2)), whole((D, D // 2))),
        out_shape=(
            jax.ShapeDtypeStruct((rows, D), BF),
            jax.ShapeDtypeStruct((rows, D), F32),
            jax.ShapeDtypeStruct((rows, D), BF),
            jax.ShapeDtypeStruct((8, D), F32),
            jax.ShapeDtypeStruct((D, D // 2), BF),
            jax.ShapeDtypeStruct((D, D // 2), BF),
        ),
        scratch_shapes=[pltpu.VMEM((rows, D), BF), pltpu.VMEM((rows, D), BF)],
        compiler_params=params(),
        cost_estimate=cost(2 * rows * D * D, 26 * rows * D),
        name="second_norm_back",
    )(place, vec, picked, grads, attended, out, back, heads)


def first_back_kernel(vec, picked, grads, carry, *refs):
    mixed = refs[: 2 * GROUPS]
    weights = refs[2 * GROUPS : 4 * GROUPS]
    values, sums = refs[4 * GROUPS :]

    @pl.when(pl.program_id(0) == 0)
    def _():
        sums[...] = jnp.zeros_like(sums)

    pulled = nt(mixed[0][...], weights[0][...])
    for left, right in zip(mixed[1:], weights[1:]):
        pulled += nt(left[...], right[...])
    unit, inverse = normalize(picked[...].astype(F32))
    grad = norm_back(pulled, unit, inverse, vec[0:1, :].astype(F32))
    values[...] = (grads[...].astype(F32) + grad + carry[...]).astype(BF)
    sums[0:1, :] += column_sum(pulled * unit)
    sums[1:2, :] += column_sum(pulled)


def first_back(vec, picked, grads, carry, mixed, weights):
    rows = picked.shape[0]
    size = 2 * PAD
    wide = pl.BlockSpec((size, D), lambda i: (i, 0))
    block = pl.BlockSpec((size, 3 * PW), lambda i: (i, 0))
    return pl.pallas_call(
        first_back_kernel,
        grid=(rows // size,),
        in_specs=[whole((16, D)), wide, wide, wide]
        + [block] * (2 * GROUPS)
        + [whole((D, 3 * PW))] * (2 * GROUPS),
        out_specs=(wide, whole((8, D))),
        out_shape=(jax.ShapeDtypeStruct((rows, D), BF), jax.ShapeDtypeStruct((8, D), F32)),
        compiler_params=params(),
        cost_estimate=cost(6 * rows * D * D, 16 * rows * D),
        name="first_norm_back",
    )(vec, picked, grads, carry, *mixed, *weights)


def put_kernel(span, places, *refs):
    half = len(refs) // 4
    sources, values, nexts, outs = (refs[i * half : (i + 1) * half] for i in range(4))
    width = places.shape[2]
    hot = lax.broadcasted_iota(jnp.int32, (span, width), 0) == places[0]
    hot = hot.astype(F32).astype(BF)
    kept = nn(hot, jnp.ones((width, 128), BF)) > 0.5
    for source, value, after, out in zip(sources, values, nexts, outs):
        moved = nn(hot[:, :PAD], value[...]) + nn(hot[:, PAD:], after[...])
        for tile in range(D // 128):
            lanes = slice(tile * 128, (tile + 1) * 128)
            out[:, lanes] = jnp.where(kept, moved[:, lanes].astype(BF), source[:, lanes])


def put(places, sources, values):
    rows = sources[0].shape[0]
    count = places.shape[0]
    span = -(-(rows // count) // 16) * 16
    block = pl.BlockSpec((span, D), lambda i: (i, 0))
    value = pl.BlockSpec((PAD, D), lambda i: (i, 0))
    after = pl.BlockSpec((16, D), lambda i: (jnp.minimum(i + 1, count - 1) * (PAD // 16), 0))
    kinds = len(sources)
    return pl.pallas_call(
        functools.partial(put_kernel, span),
        grid=(count,),
        in_specs=[pl.BlockSpec((1, 1, places.shape[2]), lambda i: (i, 0, 0))]
        + [block] * kinds
        + [value] * kinds
        + [after] * kinds,
        out_specs=(block,) * kinds,
        out_shape=(jax.ShapeDtypeStruct((rows, D), BF),) * kinds,
        compiler_params=params(),
        cost_estimate=cost(2 * kinds * rows * D * (PAD + 16), kinds * 6 * rows * D),
        name="put_rows",
    )(places, *sources, *values, *values)


def put_places(keep_slots, image_tokens):
    count = keep_slots.shape[0]
    span = -(-image_tokens // 16) * 16
    image = jnp.arange(count, dtype=jnp.int32)[:, None]
    own = keep_slots + image * (image_tokens - span)
    following = jnp.concatenate([keep_slots[1:, :16], jnp.full((1, 16), -span, jnp.int32)], axis=0)
    following = following + (image + 1) * image_tokens - image * span
    following = jnp.where(image < count - 1, following, -1)
    gap = jnp.full((count, PAD - KEEP), -1, jnp.int32)
    return jnp.concatenate([own, gap, following], axis=1)[:, None, :]


class Moves:
    def __init__(self, n_dp, n_fsdp):
        self.n_dp = n_dp
        self.n_fsdp = n_fsdp
        self.squares = n_fsdp // 2
        outer = lax.axis_index("dp")
        inner = lax.axis_index("fsdp")
        self.z = outer
        self.yx = inner // 2
        self.core = inner % 2
        self.place = jnp.stack([self.z, self.yx, self.core]).astype(jnp.int32)

    def swap(self, value, mask):
        total = self.n_dp * self.n_fsdp
        return lax.ppermute(value, AXES, [(i, i ^ mask) for i in range(total)])

    def over_z(self, values):
        return [self.swap(value, k * self.n_fsdp) for k, value in enumerate(values) if k]

    def over_yx(self, values):
        return [self.swap(value, 2 * k) for k, value in enumerate(values) if k]

    def over_core(self, value):
        return self.swap(value, 1)

    def sum_all(self, value):
        total = value
        for part in self.over_z([value] * self.n_dp):
            total = total + part
        value = total
        for part in self.over_yx([value] * self.squares):
            total = total + part
        return total + self.over_core(total)

    def along_z(self, piece):
        return place_blocks(self.place, 0, [piece] + self.over_z([piece] * self.n_dp))

    def along_yx(self, stacked):
        parts = [stacked] + self.over_yx([stacked] * self.squares)
        return place_blocks(self.place, 1, parts).reshape(-1, stacked.shape[2])


class Scatter:
    def __init__(self, moves, keeps, sends):
        self.moves = moves
        chips = moves.n_dp * moves.squares

        def shaped(value):
            return value.reshape(moves.n_dp, moves.squares, value.shape[0] // chips, value.shape[1])

        self.arrived = [shaped(moves.over_core(value)) for value in sends]
        self.keeps = [shaped(value) for value in keeps]

    def add_cores(self, place):
        blocks = add_pairs(place, self.keeps, self.arrived, self.moves.squares)
        self.squares = [[block[0]] + self.moves.over_yx(block) for block in blocks]
        return [block[0] for block in blocks]

    def add_squares(self, place):
        blocks = add_blocks(place, self.squares, self.moves.n_dp)
        self.lines = [[block[0]] + self.moves.over_z(block) for block in blocks]
        return [block[0] for block in blocks]

    def finish(self):
        results = []
        for line in self.lines:
            total = line[0].astype(F32)
            for part in line[1:]:
                total = total + part.astype(F32)
            results.append(total)
        return results


def after(value, *others):
    return lax.optimization_barrier((value, *others))[0]


def place_kernel(axis, count, place, *refs):
    out = refs[count]
    me = place[axis]
    for k in range(count):
        if axis == 0:
            out[me ^ k] = refs[k][...]
        else:
            out[:, me ^ k] = refs[k][...]


def place_blocks(place, axis, blocks):
    count = len(blocks)
    shape = blocks[0].shape
    stacked = shape[:axis] + (count,) + shape[axis:]
    return pl.pallas_call(
        functools.partial(place_kernel, axis, count),
        in_specs=[SMEM] + [pl.BlockSpec(memory_space=pltpu.VMEM)] * count,
        out_specs=pl.BlockSpec(memory_space=pltpu.VMEM),
        out_shape=jax.ShapeDtypeStruct(stacked, blocks[0].dtype),
        compiler_params=params(),
        cost_estimate=cost(0, 4 * count * math.prod(shape)),
        name="place_blocks",
    )(place, *blocks)


def add_pairs_kernel(count, place, *refs):
    for index in range(count):
        total = refs[index][...].astype(F32) + refs[count + index][...].astype(F32)
        refs[2 * count + index][...] = total[:, 0].astype(BF)


def add_pairs(place, keeps, arrived, squares):
    specs, outs, shapes, left, right = [], [], [], [], []
    for keep, other in zip(keeps, arrived):
        n_dp, _, m, n = keep.shape
        for k in range(squares):
            specs.append(
                pl.BlockSpec((n_dp, 1, m, n), lambda i, place, k=k: (0, place[1] ^ k, 0, 0))
            )
            outs.append(pl.BlockSpec((n_dp, m, n), lambda i, place: (0, 0, 0)))
            shapes.append(jax.ShapeDtypeStruct((n_dp, m, n), BF))
            left.append(keep)
            right.append(other)
    count = len(left)
    results = pl.pallas_call(
        functools.partial(add_pairs_kernel, count),
        grid_spec=pltpu.PrefetchScalarGridSpec(
            num_scalar_prefetch=1, grid=(1,), in_specs=specs + specs, out_specs=outs
        ),
        out_shape=shapes,
        compiler_params=params(),
        cost_estimate=cost(0, 6 * sum(math.prod(keep.shape) for keep in keeps)),
        name="add_cores",
    )(place, *left, *right)
    return [results[i * squares : (i + 1) * squares] for i in range(len(keeps))]


def add_blocks_kernel(count, terms, place, *refs):
    for index in range(count):
        total = refs[index * terms][...].astype(F32)
        for term in range(1, terms):
            total = total + refs[index * terms + term][...].astype(F32)
        refs[count * terms + index][...] = total[0].astype(BF)


def add_blocks(place, groups, n_dp):
    specs, outs, shapes, operands = [], [], [], []
    terms = len(groups[0])
    for arrays in groups:
        m, n = arrays[0].shape[1:]
        for k in range(n_dp):
            spec = pl.BlockSpec((1, m, n), lambda i, place, k=k: (place[0] ^ k, 0, 0))
            specs += [spec] * terms
            operands += arrays
            outs.append(pl.BlockSpec((m, n), lambda i, place: (0, 0)))
            shapes.append(jax.ShapeDtypeStruct((m, n), BF))
    results = pl.pallas_call(
        functools.partial(add_blocks_kernel, len(shapes), terms),
        grid_spec=pltpu.PrefetchScalarGridSpec(
            num_scalar_prefetch=1, grid=(1,), in_specs=specs, out_specs=outs
        ),
        out_shape=shapes,
        compiler_params=params(),
        cost_estimate=cost(0, 4 * sum(math.prod(a.shape) for g in groups for a in g)),
        name="add_squares",
    )(place, *operands)
    return [results[i * n_dp : (i + 1) * n_dp] for i in range(len(groups))]


def adam_update(master, grad, first, second, rate, decay):
    first_new = first_beta * first + (1.0 - first_beta) * grad
    second_new = second_beta * second + (1.0 - second_beta) * grad * grad
    first_hat = first_new / (1.0 - first_beta**STEP)
    second_hat = second_new / (1.0 - second_beta**STEP)
    updated = master - rate * (first_hat / (jnp.sqrt(second_hat) + adam_eps) + decay * master)
    return (first_new, second_new, updated)


def on_device(
    n_dp,
    n_fsdp,
    tokens,
    keep_slots,
    cotangent,
    project_in,
    project_out,
    expand,
    contract,
    vectors,
    first_in,
    first_out,
    first_expand,
    first_contract,
    first_vectors,
    second_in,
    second_out,
    second_expand,
    second_contract,
    second_vectors,
):
    moves = Moves(n_dp, n_fsdp)
    place, core = moves.place, moves.core
    total = n_dp * n_fsdp
    chips = total // 2
    rows_in = project_in.shape[0]
    units = contract.shape[0]
    per_chunk = units // CHUNKS
    owner = moves.z * n_fsdp + lax.axis_index("fsdp")

    columns = vectors.shape[1]
    padded = jnp.pad(vectors.astype(BF), ((0, 16 - vectors.shape[0]), (0, 0)))
    vec = lax.dynamic_update_slice(jnp.zeros((16, D), BF), padded, (0, owner * columns))
    vec = moves.sum_all(vec)

    def pair_columns(value, pair):
        return [value[:, part * D + pair * PW : part * D + (pair + 1) * PW] for part in range(3)]

    low_in = project_in.astype(BF)
    low_out = project_out.astype(BF)
    low_up = expand.astype(BF).reshape(rows_in, chips, 2, CHUNKS, per_chunk)
    low_up = low_up.transpose(0, 3, 2, 1, 4).reshape(rows_in, CHUNKS, 2, HALF)
    low_down = contract.astype(BF)
    halves = []
    for parity in range(2):
        parts = []
        for group in range(GROUPS):
            parts += pair_columns(low_in, 2 * group + parity)
        parts.append(low_out[:, parity * (D // 2) : (parity + 1) * (D // 2)])
        parts += [low_up[:, chunk, parity] for chunk in range(CHUNKS)]
        halves.append(jnp.concatenate(parts, axis=1))
    mine = jnp.where(core == 0, halves[0], halves[1])
    theirs = jnp.where(core == 0, halves[1], halves[0])
    arrived = moves.over_core(theirs)
    rows = jnp.where(
        core == 0,
        jnp.concatenate([mine, arrived], axis=0),
        jnp.concatenate([arrived, mine], axis=0),
    )

    step = 3 * PW
    at = GROUPS * step
    pieces = [rows[:, group * step : (group + 1) * step] for group in range(GROUPS - 1)]
    pieces.append(rows[:, (GROUPS - 1) * step : at + D // 2])
    at += D // 2
    for chunk in range(CHUNKS):
        pieces.append(rows[:, at + chunk * HALF : at + (chunk + 1) * HALF])
        pieces.append(low_down[chunk * per_chunk : (chunk + 1) * per_chunk])
    stacked = []
    for index, piece in enumerate(pieces):
        if index:
            piece = after(piece, stacked[-1])
        stacked.append(moves.along_z(piece))
    gathered = []
    for index, stack in enumerate(stacked):
        if index:
            stack = after(stack, gathered[-1][0])
        own = moves.along_yx(stack)
        gathered.append((own, moves.over_core(own)))
    w_in = gathered[: GROUPS - 1]
    w_in.append(tuple(value[:, :step] for value in gathered[GROUPS - 1]))
    w_out = tuple(value[:, step:] for value in gathered[GROUPS - 1])
    w_up = gathered[GROUPS::2]
    w_down = gathered[GROUPS + 1 :: 2]

    count = keep_slots.shape[0]
    image_tokens = tokens.shape[0] // count
    slots = jnp.pad(keep_slots, ((0, 0), (0, PAD - KEEP)), constant_values=-4 * image_tokens)
    picked, grad_rows, normed_one, grad_mlp = pick(tokens, cotangent, slots[:, :, None], vec)
    mask = local_mask()
    mixed, heads = [], []
    for group in range(GROUPS):
        mixed_own, mixed_other, heads_own, heads_other = heads_forward(
            group, after(place, *heads[-1:]), mask, vec, normed_one, *w_in[group]
        )
        mixed.append((mixed_own, mixed_other))
        heads += [heads_own, heads_other]
    attended, normed_two, heads_out, w_out_full = mix(place, vec, picked, *w_out, heads)

    bias = vec[9:13].astype(F32).reshape(chips, 2, CHUNKS, per_chunk)
    bias = bias.transpose(2, 1, 0, 3).reshape(CHUNKS * 2, 1, HALF)
    sums, up_down, bias_sums = (), [], []
    here = place
    for chunk in range(CHUNKS):
        own_up, other_up = w_up[chunk]
        own_down, other_down = w_down[chunk]
        result = mlp(
            chunk,
            here,
            bias,
            normed_two,
            grad_mlp,
            (other_up, other_down, own_up, own_down),
            sums,
        )
        sums = result[:2]
        gw1_other, gw2_other, gw1_own, gw2_own, hidden_sums = result[2:]
        up_down.append(Scatter(moves, [gw1_own, gw2_own], [gw1_other, gw2_other]))
        bias_sums.append(hidden_sums)
        if chunk == 0:
            here = after(place, *up_down[0].add_cores(place))

    here = after(place, *up_down[0].add_squares(after(place, sums[0])))
    grad_attended, carry, put_values, turn_sums, gw_own, gw_other = turn(
        here, vec, picked, grad_rows, attended, *sums, heads_out
    )
    here = after(place, *up_down[1].add_cores(after(place, grad_attended)))
    sum_in, grad_mixed, mixed_sums = [], [], []
    out_keep, out_send = gw_own, gw_other
    for group in range(GROUPS):
        gm_own, gm_other, gw_own, gw_other, sums_own, sums_other = heads_backward(
            group, here, mask, grad_attended, normed_one, w_out_full, *mixed[group]
        )
        grad_mixed += [gm_own, gm_other]
        if group == 0:
            sum_in.append(Scatter(moves, [out_keep, gw_own], [out_send, gw_other]))
            here = after(place, gm_own)
        else:
            sum_in.append(Scatter(moves, [gw_own], [gw_other]))
            done = sum_in[group - 1].add_cores(after(place, gm_own))
            if group == 1:
                done += up_down[1].add_squares(after(place, gm_own))
            else:
                done += sum_in[group - 2].add_squares(after(place, gm_own))
            here = after(place, *done)
        in_order = jnp.where(
            core == 0,
            jnp.stack([sums_own[0], sums_other[0]]),
            jnp.stack([sums_other[0], sums_own[0]]),
        )
        mixed_sums.append(in_order.reshape(2, 3, PW))
    grad_values, first_sums = first_back(
        after(vec, here),
        picked,
        grad_rows,
        carry,
        grad_mixed,
        [weight for pair in w_in for weight in pair],
    )
    done = sum_in[1].add_squares(after(place, grad_values))
    done += sum_in[2].add_cores(after(place, grad_values))
    places = put_places(keep_slots, image_tokens)
    (activations,) = put(after(places, *done), (tokens,), (put_values,))
    done = sum_in[2].add_squares(after(place, activations))
    (input_grad,) = put(after(places, *done), (cotangent,), (grad_values,))
    up_down = [part.finish() for part in up_down]
    sum_in = [part.finish() for part in sum_in]
    sum_out = sum_in[0][0]
    sum_in = [part[-1] for part in sum_in]

    mixed_sums = jnp.concatenate(mixed_sums, axis=0)
    grad_bias = jnp.concatenate(bias_sums, axis=0).reshape(CHUNKS, 2, chips, per_chunk)
    local_squares = jnp.zeros((), F32)
    for piece in sum_in + [sum_out] + [part for pair in up_down for part in pair]:
        local_squares = local_squares + jnp.sum(piece * piece)
    table = jnp.concatenate(
        [
            first_sums[0:2],
            mixed_sums[:, 0].reshape(1, D),
            mixed_sums[:, 2].reshape(1, D),
            turn_sums[0:5],
            grad_bias.transpose(2, 1, 0, 3).reshape(4, D),
            jnp.broadcast_to(local_squares, (3, D)),
        ],
        axis=0,
    )
    table = moves.sum_all(table)
    grad_vectors = table[:13]
    total_squares = table[13, 0] + jnp.sum(grad_vectors * grad_vectors)
    grad_norm = jnp.sqrt(total_squares)
    factor = jnp.minimum(1.0, clip_share * math.sqrt(PARAMS) / (grad_norm + 1e-06))

    def owned(value):
        return lax.dynamic_slice_in_dim(value, core * rows_in, rows_in, axis=0)

    def others(value):
        return lax.dynamic_slice_in_dim(value, (1 - core) * rows_in, rows_in, axis=0)

    def ordered(mine, theirs):
        return jnp.where(core == 0, jnp.stack([mine, theirs]), jnp.stack([theirs, mine]))

    ups = jnp.concatenate([pair[0] for pair in up_down], axis=1)
    ups = ordered(owned(ups), moves.over_core(others(ups)))
    ups = ups.reshape(2, rows_in, CHUNKS, chips, per_chunk)
    summed_expand = ups.transpose(1, 3, 0, 2, 4).reshape(rows_in, HIDDEN)
    summed_contract = jnp.concatenate([pair[1] for pair in up_down], axis=0)
    ins = jnp.concatenate(sum_in + [sum_out], axis=1)
    ins = ordered(owned(ins), moves.over_core(others(ins)))
    sum_ins = ins[:, :, : GROUPS * step].reshape(2, rows_in, GROUPS, 3, PW)
    summed_in = sum_ins.transpose(1, 3, 2, 0, 4).reshape(rows_in, 3 * D)
    summed_out = ins[:, :, GROUPS * step :].transpose(1, 0, 2).reshape(rows_in, D)
    summed_vectors = lax.dynamic_slice_in_dim(grad_vectors, owner * columns, columns, axis=1)

    summed = (summed_in, summed_out, summed_expand, summed_contract, summed_vectors)
    masters = (project_in, project_out, expand, contract, vectors)
    firsts = (first_in, first_out, first_expand, first_contract, first_vectors)
    seconds = (second_in, second_out, second_expand, second_contract, second_vectors)
    rates = (matrix_rate, matrix_rate, matrix_rate, matrix_rate, vector_rate)
    decays = (matrix_decay, matrix_decay, matrix_decay, matrix_decay, 0.0)
    results = [
        adam_update(
            masters[index],
            summed[index] * factor,
            firsts[index],
            seconds[index],
            rates[index],
            decays[index],
        )
        for index in range(5)
    ]
    momenta = tuple(item[0] for item in results)
    variances = tuple(item[1] for item in results)
    updated = tuple(item[2] for item in results)
    copies = tuple(item.astype(BF) for item in updated)
    return (
        (activations, input_grad, grad_norm.reshape(1)) + momenta + variances + updated + copies
    )


def solution(mesh):
    split = P(AXES, None)
    columns = P(None, AXES)
    weights = (split, split, split, split, columns)
    return jax.shard_map(
        functools.partial(on_device, mesh.shape["dp"], mesh.shape["fsdp"]),
        mesh=mesh,
        in_specs=(split, split, split) + weights * 3,
        out_specs=(split, split, P()) + weights * 4,
        check_vma=False,
    )
```

time: 1180 us -> 668 us (0.57); the launches traced: 1160 us -> 662 us
  Pallas kernels: 0 us -> 383 us
  matrix products: 312 us -> 0 us
  local copies, waits for them, and re-layouts: 296 us -> 35.8 us
  waiting for transfers between devices: 232 us -> 73.1 us
  other arithmetic: 179 us -> 20.7 us
  starting transfers between devices: 0.74 us -> 140 us
  blocking collectives: 121 us -> 0 us
    pallas_call x0 -> x38, Pallas kernels: none -> 383 us  [the longest x2 98.5 us: mlp(): pl.pallas_call(functools.partial(mlp_kernel, chunk, steps, size), grid=(s...]
    dot_general x26 -> x0, matrix products: 312 us -> none  [the longest x1 72.8 us: on_device(): jnp.dot(normed_two_low, full[2], preferred_element_type=jnp.float32)]
    reduce_scatter x4 -> x0, waiting for transfers between devices: 232 us -> none  [the longest x1 139 us: on_device(): lax.psum_scatter(grad_contract, ('dp', 'fsdp'), scatter_dimension=0, tile...]
    reshape x36 -> x9, local copies, waits for them, and re-layouts: 159 us -> 4.56 us  [the longest x2 2.1 us: on_device(): jnp.concatenate(bias_sums, axis=0).reshape(CHUNKS, 2, chips, per_chunk)]
    ppermute x0 -> x122, starting transfers between devices: none -> 140 us  [swap(): return lax.ppermute(value, AXES, [(i, i ^ mask) for i in range(total)])]
    ppermute x0 -> x122, waiting for transfers between devices: none -> 73.1 us  [swap(): return lax.ppermute(value, AXES, [(i, i ^ mask) for i in range(total)])]
    scatter-add x2 -> x0, other arithmetic: 65.5 us -> none  [the longest x1 32.8 us: on_device(): tokens.astype(jnp.float32).at[rows].add(branch * routed[:, None])]
    slice x19 -> x13, local copies, waits for them, and re-layouts: 63 us -> 8.47 us  [the longest x2 3.54 us: on_device(): w_in.append(tuple((value[:, :step] for value in gathered[GROUPS - 1])))]
  transfers between devices with their start and end apart: 8 -> 122, of which waited for: 2 -> 32; matrix products, arithmetic and copies ran while one was open for 45% -> 5% of each run, Pallas kernels for 0% -> 53%
where the time goes in v1:
time: 668 us; the launch traced here: 662 us
  Pallas kernels  383 us (57%)
  starting transfers between devices  140 us (21%)
  waiting for transfers between devices  73.1 us (11%)
  local copies, waits for them, and re-layouts  35.8 us (5%)
  other arithmetic  20.7 us (3%)
  between operations  10.3 us (2%)
    ppermute x122, starting transfers between devices, swap(): return lax.ppermute(value, AXES, [(i, i ^ mask) for i in range(total)])  140 us
    pallas_call x2, Pallas kernels, mlp(): pl.pallas_call(functools.partial(mlp_kernel, chunk, steps, size), grid=(s...  98.5 us
    pallas_call x3, Pallas kernels, heads_backward(): pl.pallas_call(functools.partial(heads_back_kernel, group, count), grid=(...  80.4 us
    ppermute x122, waiting for transfers between devices, swap(): return lax.ppermute(value, AXES, [(i, i ^ mask) for i in range(total)])  73.1 us
    pallas_call x3, Pallas kernels, heads_forward(): pl.pallas_call(functools.partial(heads_kernel, group), grid=(count,), in_...  50.3 us
    pallas_call x14, Pallas kernels, place_blocks(): pl.pallas_call(functools.partial(place_kernel, axis, count), in_specs=[SM...  27.6 us
    pallas_call x2, Pallas kernels, put(): pl.pallas_call(functools.partial(put_kernel, span), grid=(count,), in_spe...  23.8 us
    pallas_call x1, Pallas kernels, turn(): pl.pallas_call(functools.partial(turn_kernel, steps, size), grid=(steps +...  23.1 us
  transfers between devices with their start and end apart: 122, of which 32 were waited for; matrix products, arithmetic and copies ran while one was open for 5% of the time, Pallas kernels for 53%

profile of v1, /device:TPU:0, one launch (start us, length us, event | category | flops | bytes accessed | tf_op | source)
XLA Modules:
  0.0 662.2 jit_solution(13158952405992474461)
XLA Ops:
  6.2 5.0 collective-permute-start.10
  41.5 3.7 collective-permute-done.15.refs_2_
  63.6 5.6 collective-permute-done.31.refs_3_
  116.3 14.9 %pick_rows.1 = (bf16[2176,768]{1,0:T(8,128)(2,1)}, bf16[2176,768]{1,0:T(8,128)(2,1)}, bf16[2176,768]{1,0:T(8,128)(2,1)}, bf16[2176,768]{1,0:T(8,128)(2,1)}) custom-call(s32[8,272,1]{2,1,0:T(8,128)} %copy.52.slots, bf16[16,768]{1,0:T(8,128)(2,1)} %add.328.vec, bf16[4336,768]{1,0:T(8,128)(2,1)} %refs_0_.2, bf16[4336,768]{1,0:T(8,128)(2,1)} %refs_0_.3), custom_call_target="tpu_custom_call" | custom-call | flops 3743416320 | bytes 26689536 | tf_op jit(solution)/shard_map/pick_rows/pallas_call | solution.py:131
  146.8 16.8 %attention_0.1 = (bf16[2176,384]{1,0:T(8,128)(2,1)}, bf16[2176,384]{1,0:T(8,128)(2,1)}, bf16[2176,128]{1,0:T(8,128)(2,1)}, bf16[2176,128]{1,0:T(8,128)(2,1)}) custom-call(s32[3]{0:T(128)} %pad_add_fusion.1.place, f32[80,160]{1,0:T(8,128)} %pad_maximum_fusion.1.mask, bf16[16,768]{1,0:T(8,128)(2,1)} %add.328.vec, bf16[2176,768]{1,0:T(8,128)(2,1)} %get-tuple-element.180.normed, ...), custom_call_target="tpu_custom_call" | custom-call | flops 3002114048 | bytes 13369344 | tf_op jit(solution)/shard_map/attention_0/pallas_call | solution.py:268
  163.6 16.8 %attention_1.1 = (bf16[2176,384]{1,0:T(8,128)(2,1)}, bf16[2176,384]{1,0:T(8,128)(2,1)}, bf16[2176,128]{1,0:T(8,128)(2,1)}, bf16[2176,128]{1,0:T(8,128)(2,1)}) custom-call(s32[3]{0:T(128)} %pad_add_fusion.1.place, f32[80,160]{1,0:T(8,128)} %pad_maximum_fusion.1.mask, bf16[16,768]{1,0:T(8,128)(2,1)} %add.328.vec, bf16[2176,768]{1,0:T(8,128)(2,1)} %get-tuple-element.180.normed, ...), custom_call_target="tpu_custom_call" | custom-call | flops 3002114048 | bytes 13369344 | tf_op jit(solution)/shard_map/attention_1/pallas_call | solution.py:268
  190.1 16.7 %attention_2.1 = (bf16[2176,384]{1,0:T(8,128)(2,1)}, bf16[2176,384]{1,0:T(8,128)(2,1)}, bf16[2176,128]{1,0:T(8,128)(2,1)}, bf16[2176,128]{1,0:T(8,128)(2,1)}) custom-call(s32[3]{0:T(128)} %pad_add_fusion.1.place, f32[80,160]{1,0:T(8,128)} %pad_maximum_fusion.1.mask, bf16[16,768]{1,0:T(8,128)(2,1)} %add.328.vec, bf16[2176,768]{1,0:T(8,128)(2,1)} %get-tuple-element.180.normed, ...), custom_call_target="tpu_custom_call" | custom-call | flops 3002114048 | bytes 13369344 | tf_op jit(solution)/shard_map/attention_2/pallas_call | solution.py:268
  206.8 11.1 %project_and_norm.1 = (f32[2176,768]{1,0:T(8,128)}, bf16[2176,768]{1,0:T(8,128)(2,1)}, bf16[2176,768]{1,0:T(8,128)(2,1)}, bf16[768,768]{1,0:T(8,128)(2,1)}) custom-call(s32[3]{0:T(128)} %pad_add_fusion.1.place, bf16[16,768]{1,0:T(8,128)(2,1)} %add.328.vec, bf16[2176,768]{1,0:T(8,128)(2,1)} %get-tuple-element.174.picked, ...), custom_call_target="tpu_custom_call" | custom-call | flops 2566914048 | bytes 20054016 | tf_op jit(solution)/shard_map/project_and_norm/pallas_call | solution.py:381
  217.9 48.5 %feed_forward_0.1 = (f32[2176,768]{1,0:T(8,128)}, f32[2176,768]{1,0:T(8,128)}, bf16[768,768]{1,0:T(8,128)(2,1)}, bf16[768,768]{1,0:T(8,128)(2,1)}, bf16[768,768]...) custom-call(s32[3]{0:T(128)} %pad_add_fusion.1.place, f32[4,1,768]{2,1,0:T(1,128)} %reshape.269.bias, ...), custom_call_target="tpu_custom_call" | custom-call | flops 30802968576 | bytes 29491200 | tf_op jit(solution)/shard_map/feed_forward_0/pallas_call | solution.py:503
  274.0 4.5 add_cores.5
  282.0 50.0 %feed_forward_1.1 = (f32[2176,768]{1,0:T(8,128)}, f32[2176,768]{1,0:T(8,128)}, bf16[768,768]{1,0:T(8,128)(2,1)}, bf16[768,768]{1,0:T(8,128)(2,1)}, bf16[768,768]...) custom-call(s32[3]{0:T(128)} %pad_add_fusion.1.place, f32[4,1,768]{2,1,0:T(1,128)} %reshape.269.bias, ...), custom_call_target="tpu_custom_call" | custom-call | flops 30802968576 | bytes 29491200 | tf_op jit(solution)/shard_map/feed_forward_1/pallas_call | solution.py:503
  342.7 5.0 collective-permute-done.63.refs_18_.refs_22_.refs_26_.refs_30_
  357.3 23.1 %second_norm_back.1 = (bf16[2176,768]{1,0:T(8,128)(2,1)}, f32[2176,768]{1,0:T(8,128)}, bf16[2176,768]{1,0:T(8,128)(2,1)}, f32[8,768]{1,0:T(8,128)}, bf16[768,384]{1,0:T(8,128)(2,1)}, /*index=5*/bf16[768,384]{1,0:T(8,128)(2,1)}) custom-call(s32[3]{0:T(128)} %pad_add_fusion.1.place, bf16[16,768]{1,0:T(8,128)(2,1)} %add.328.vec, ...), custom_call_target="tpu_custom_call" | custom-call | flops 2566914048 | bytes 43450368 | tf_op jit(solution)/shard_map/second_norm_back/pallas_call | solution.py:582
  391.0 4.5 add_cores.6
  395.5 26.7 %attention_back_0.1 = (bf16[2176,384]{1,0:T(8,128)(2,1)}, bf16[2176,384]{1,0:T(8,128)(2,1)}, bf16[768,384]{1,0:T(8,128)(2,1)}, bf16[768,384]{1,0:T(8,128)(2,1)}, f32[8,384]{1,0:T(8,128)}, /*index=5*/f32[8,384]{1,0:T(8,128)}) custom-call(s32[3]{0:T(128)} %pad_add_fusion.1.place, f32[80,160]{1,0:T(8,128)} %pad_maximum_fusion.1.mask, ...), custom_call_target="tpu_custom_call" | custom-call | flops 4510552064 | bytes 20054016 | tf_op jit(solution)/shard_map/attention_back_0/pallas_call | solution.py:335
  423.3 27.0 %attention_back_1.1 = (bf16[2176,384]{1,0:T(8,128)(2,1)}, bf16[2176,384]{1,0:T(8,128)(2,1)}, bf16[768,384]{1,0:T(8,128)(2,1)}, bf16[768,384]{1,0:T(8,128)(2,1)}, f32[8,384]{1,0:T(8,128)}, /*index=5*/f32[8,384]{1,0:T(8,128)}) custom-call(s32[3]{0:T(128)} %pad_add_fusion.1.place, f32[80,160]{1,0:T(8,128)} %pad_maximum_fusion.1.mask, ...), custom_call_target="tpu_custom_call" | custom-call | flops 4510552064 | bytes 20054016 | tf_op jit(solution)/shard_map/attention_back_1/pallas_call | solution.py:335
  459.4 7.8 %collective-permute-done.70.refs_2_.refs_6_.refs_10_.refs_14_ = bf16[4,48,768]{2,1,0:T(8,128)(2,1)S(1)} collective-permute-done((bf16[4,48,768]{2,1,0:T(8,128)(2,1)S(1)}, bf16[4,48,768]{2,1,0:T(8,128)(2,1)S(1)}, u32[]{:S(2)}, u32[]{:S(2)}) %collective-permute-start.70) | collective-permute-done | bytes 294944 | tf_op jit(solution)/shard_map/ppermute | solution.py:703
  467.7 6.9 %collective-permute-done.73.refs_18_.refs_22_.refs_26_.refs_30_ = bf16[4,48,768]{2,1,0:T(8,128)(2,1)S(1)} collective-permute-done((bf16[4,48,768]{2,1,0:T(8,128)(2,1)S(1)}, bf16[4,48,768]{2,1,0:T(8,128)(2,1)S(1)}, u32[]{:S(2)}, u32[]{:S(2)}) %collective-permute-start.73) | collective-permute-done | bytes 294944 | tf_op jit(solution)/shard_map/ppermute | solution.py:703
  497.1 3.4 add_cores.7
  505.6 26.7 %attention_back_2.1 = (bf16[2176,384]{1,0:T(8,128)(2,1)}, bf16[2176,384]{1,0:T(8,128)(2,1)}, bf16[768,384]{1,0:T(8,128)(2,1)}, bf16[768,384]{1,0:T(8,128)(2,1)}, f32[8,384]{1,0:T(8,128)}, /*index=5*/f32[8,384]{1,0:T(8,128)}) custom-call(s32[3]{0:T(128)} %pad_add_fusion.1.place, f32[80,160]{1,0:T(8,128)} %pad_maximum_fusion.1.mask, ...), custom_call_target="tpu_custom_call" | custom-call | flops 4510552064 | bytes 20054016 | tf_op jit(solution)/shard_map/attention_back_2/pallas_call | solution.py:335
  532.5 20.4 %first_norm_back.1 = (bf16[2176,768]{1,0:T(8,128)(2,1)}, f32[8,768]{1,0:T(8,128)}) custom-call(bf16[16,768]{1,0:T(8,128)(2,1)} %add.328.vec, bf16[2176,768]{1,0:T(8,128)(2,1)} %get-tuple-element.174.picked, bf16[2176,768]{1,0:T(8,128)(2,1)} %get-tuple-element.175.grads, f32[2176,768]{1,0:T(8,128)} %get-tuple-element.222.carry, ...), custom_call_target="tpu_custom_call" | custom-call | flops 7700742144 | bytes 26738688 | tf_op jit(solution)/shard_map/first_norm_back/pallas_call | solution.py:626
  590.8 3.4 collective-permute-done.80.refs_1_.refs_5_.refs_9_.refs_13_
  595.6 11.9 %put_rows.2 = bf16[4336,768]{1,0:T(8,128)(2,1)} custom-call(s32[8,1,288]{2,1,0:T(1,128)} %broadcast_in_dim.44.places, bf16[4336,768]{1,0:T(8,128)(2,1)} %refs_0_.2, bf16[2176,768]{1,0:T(8,128)(2,1)} %get-tuple-element.276.refs_1_.refs_2_, bf16[2176,768]{1,0:T(8,128)(2,1)} %get-tuple-element.276.refs_1_.refs_2_), custom_call_target="tpu_custom_call" | custom-call | flops 1918107648 | bytes 19980288 | tf_op jit(solution)/shard_map/put_rows/pallas_call | solution.py:662
  628.7 11.9 %put_rows.3 = bf16[4336,768]{1,0:T(8,128)(2,1)} custom-call(s32[8,1,288]{2,1,0:T(1,128)} %broadcast_in_dim.44.places, bf16[4336,768]{1,0:T(8,128)(2,1)} %refs_0_.3, bf16[2176,768]{1,0:T(8,128)(2,1)} %get-tuple-element.262.refs_1_.refs_2_, bf16[2176,768]{1,0:T(8,128)(2,1)} %get-tuple-element.262.refs_1_.refs_2_), custom_call_target="tpu_custom_call" | custom-call | flops 1918107648 | bytes 19980288 | tf_op jit(solution)/shard_map/put_rows/pallas_call | solution.py:662
  (610 shorter events, 279.6 us)
Async XLA Ops:
  111.7 32.2 %collective-permute-start.27 = (bf16[768,384]{1,0:T(8,128)(2,1)}, bf16[768,384]{1,0:T(8,128)(2,1)}, u32[]{:S(2)}, u32[]{:S(2)}) collective-permute-start(bf16[768,384]{1,0:T(8,128)(2,1)} %bitcast.10.own_w.refs_6_), channel_id=1, source_target_pairs={{0,1},{1,0},{2,3},{3,2},{4,5},{5,4},{6,7},{7,6},{8,9},{9,8},{10,11... | collective-permute-start | bytes 1769480 | tf_op jit(solution)/shard_map/ppermute | solution.py:703
  111.7 33.7 %collective-permute-start.28 = (bf16[768,384]{1,0:T(8,128)(2,1)}, bf16[768,384]{1,0:T(8,128)(2,1)}, u32[]{:S(2)}, u32[]{:S(2)}) collective-permute-start(bf16[768,384]{1,0:T(8,128)(2,1)} %bitcast.11.own_w.refs_8_), channel_id=1, source_target_pairs={{0,1},{1,0},{2,3},{3,2},{4,5},{5,4},{6,7},{7,6},{8,9},{9,8},{10,11... | collective-permute-start | bytes 1769480 | tf_op jit(solution)/shard_map/ppermute | solution.py:703
  116.2 70.1 %collective-permute-start.26 = (bf16[768,768]{1,0:T(8,128)(2,1)S(1)}, bf16[768,768]{1,0:T(8,128)(2,1)}, u32[]{:S(2)}, u32[]{:S(2)}) collective-permute-start(bf16[768,768]{1,0:T(8,128)(2,1)S(1)} %bitcast.144), channel_id=1, source_target_pairs={{0,1},{1,0},{2,3},{3,2},{4,5},{5,4},{6,7},{7,6},{8,9},{9,8},{10,11... | collective-permute-start | bytes 3538952 | tf_op jit(solution)/shard_map/ppermute | solution.py:703
  143.9 74.0 %collective-permute-start.35 = (bf16[768,768]{1,0:T(8,128)(2,1)S(1)}, bf16[768,768]{1,0:T(8,128)(2,1)}, u32[]{:S(2)}, u32[]{:S(2)}) collective-permute-start(bf16[768,768]{1,0:T(8,128)(2,1)S(1)} %bitcast.148), channel_id=1, source_target_pairs={{0,1},{1,0},{2,3},{3,2},{4,5},{5,4},{6,7},{7,6},{8,9},{9,8},{10,11... | collective-permute-start | bytes 3538952 | tf_op jit(solution)/shard_map/ppermute | solution.py:703
  143.9 36.5 %collective-permute-start.49 = (bf16[4,48,768]{2,1,0:T(8,128)(2,1)S(1)}, bf16[4,48,768]{2,1,0:T(8,128)(2,1)S(1)}, u32[]{:S(2)}, u32[]{:S(2)}) collective-permute-start(bf16[4,48,768]{2,1,0:T(8,128)(2,1)S(1)} %copy-done.36), channel_id=1, source_target_pairs={{0,4},{1,5},{2,6},{3,7},{4,0},{5,1},{6,2},{7,3},{8,12},{9,13},{10,... | collective-permute-start | bytes 884744 | tf_op jit(solution)/shard_map/ppermute | solution.py:703
  145.4 35.0 %collective-permute-start.50 = (bf16[4,48,768]{2,1,0:T(8,128)(2,1)S(1)}, bf16[4,48,768]{2,1,0:T(8,128)(2,1)S(1)}, u32[]{:S(2)}, u32[]{:S(2)}) collective-permute-start(bf16[4,48,768]{2,1,0:T(8,128)(2,1)S(1)} %copy-done.36), channel_id=1, source_target_pairs={{0,6},{1,7},{2,4},{3,5},{4,2},{5,3},{6,0},{7,1},{8,14},{9,15},{10,... | collective-permute-start | bytes 884744 | tf_op jit(solution)/shard_map/ppermute | solution.py:703
  146.8 71.1 %collective-permute-start.42 = (bf16[768,768]{1,0:T(8,128)(2,1)}, bf16[768,768]{1,0:T(8,128)(2,1)}, u32[]{:S(2)}, u32[]{:S(2)}) collective-permute-start(bf16[768,768]{1,0:T(8,128)(2,1)} %bitcast.14.refs_3_), channel_id=1, source_target_pairs={{0,1},{1,0},{2,3},{3,2},{4,5},{5,4},{6,7},{7,6},{8,9},{9,8},{10,11... | collective-permute-start | bytes 3538952 | tf_op jit(solution)/shard_map/ppermute | solution.py:703
  184.2 82.8 %collective-permute-start.55 = (bf16[4,48,768]{2,1,0:T(8,128)(2,1)S(1)}, bf16[4,48,768]{2,1,0:T(8,128)(2,1)S(1)}, u32[]{:S(2)}, u32[]{:S(2)}) collective-permute-start(bf16[4,48,768]{2,1,0:T(8,128)(2,1)S(1)} %copy-done.34), channel_id=1, source_target_pairs={{0,2},{1,3},{2,0},{3,1},{4,6},{5,7},{6,4},{7,5},{8,10},{9,11},{10,... | collective-permute-start | bytes 884744 | tf_op jit(solution)/shard_map/ppermute | solution.py:703
  184.9 82.2 %collective-permute-start.56 = (bf16[4,48,768]{2,1,0:T(8,128)(2,1)S(1)}, bf16[4,48,768]{2,1,0:T(8,128)(2,1)}, u32[]{:S(2)}, u32[]{:S(2)}) collective-permute-start(bf16[4,48,768]{2,1,0:T(8,128)(2,1)S(1)} %copy-done.34), channel_id=1, source_target_pairs={{0,4},{1,5},{2,6},{3,7},{4,0},{5,1},{6,2},{7,3},{8,12},{9,13},{10,... | collective-permute-start | bytes 884744 | tf_op jit(solution)/shard_map/ppermute | solution.py:703
  186.3 80.8 %collective-permute-start.57 = (bf16[4,48,768]{2,1,0:T(8,128)(2,1)S(1)}, bf16[4,48,768]{2,1,0:T(8,128)(2,1)}, u32[]{:S(2)}, u32[]{:S(2)}) collective-permute-start(bf16[4,48,768]{2,1,0:T(8,128)(2,1)S(1)} %copy-done.34), channel_id=1, source_target_pairs={{0,6},{1,7},{2,4},{3,5},{4,2},{5,3},{6,0},{7,1},{8,14},{9,15},{10,... | collective-permute-start | bytes 884744 | tf_op jit(solution)/shard_map/ppermute | solution.py:703
  278.5 54.1 %collective-permute-start.59 = (bf16[4,48,768]{2,1,0:T(8,128)(2,1)}, bf16[4,48,768]{2,1,0:T(8,128)(2,1)S(1)}, u32[]{:S(2)}, u32[]{:S(2)}) collective-permute-start(bf16[4,48,768]{2,1,0:T(8,128)(2,1)} %get-tuple-element.210), channel_id=1, source_target_pairs={{0,2},{1,3},{2,0},{3,1},{4,6},{5,7},{6,4},{7,5},{8,10},{9,11},{10,... | collective-permute-start | bytes 884744 | tf_op jit(solution)/shard_map/ppermute | solution.py:703
  279.1 54.2 %collective-permute-start.60 = (bf16[4,48,768]{2,1,0:T(8,128)(2,1)}, bf16[4,48,768]{2,1,0:T(8,128)(2,1)S(1)}, u32[]{:S(2)}, u32[]{:S(2)}) collective-permute-start(bf16[4,48,768]{2,1,0:T(8,128)(2,1)} %get-tuple-element.211), channel_id=1, source_target_pairs={{0,4},{1,5},{2,6},{3,7},{4,0},{5,1},{6,2},{7,3},{8,12},{9,13},{10,... | collective-permute-start | bytes 884744 | tf_op jit(solution)/shard_map/ppermute | solution.py:703
  280.6 54.2 %collective-permute-start.61 = (bf16[4,48,768]{2,1,0:T(8,128)(2,1)}, bf16[4,48,768]{2,1,0:T(8,128)(2,1)S(1)}, u32[]{:S(2)}, u32[]{:S(2)}) collective-permute-start(bf16[4,48,768]{2,1,0:T(8,128)(2,1)} %get-tuple-element.212), channel_id=1, source_target_pairs={{0,6},{1,7},{2,4},{3,5},{4,2},{5,3},{6,0},{7,1},{8,14},{9,15},{10,... | collective-permute-start | bytes 884744 | tf_op jit(solution)/shard_map/ppermute | solution.py:703
  332.0 57.7 %collective-permute-start.65 = (bf16[768,768]{1,0:T(8,128)(2,1)}, bf16[768,768]{1,0:T(8,128)(2,1)S(1)}, u32[]{:S(2)}, u32[]{:S(2)}) collective-permute-start(bf16[768,768]{1,0:T(8,128)(2,1)} %get-tuple-element.227), channel_id=1, source_target_pairs={{0,1},{1,0},{2,3},{3,2},{4,5},{5,4},{6,7},{7,6},{8,9},{9,8},{10,11... | collective-permute-start | bytes 3538952 | tf_op jit(solution)/shard_map/ppermute | solution.py:703
  332.1 57.6 %collective-permute-start.66 = (bf16[768,768]{1,0:T(8,128)(2,1)}, bf16[768,768]{1,0:T(8,128)(2,1)S(1)}, u32[]{:S(2)}, u32[]{:S(2)}) collective-permute-start(bf16[768,768]{1,0:T(8,128)(2,1)} %get-tuple-element.228), channel_id=1, source_target_pairs={{0,1},{1,0},{2,3},{3,2},{4,5},{5,4},{6,7},{7,6},{8,9},{9,8},{10,11... | collective-permute-start | bytes 3538952 | tf_op jit(solution)/shard_map/ppermute | solution.py:703
  422.3 33.6 %collective-permute-start.69 = (bf16[4,48,768]{2,1,0:T(8,128)(2,1)S(1)}, bf16[4,48,768]{2,1,0:T(8,128)(2,1)S(1)}, u32[]{:S(2)}, u32[]{:S(2)}) collective-permute-start(bf16[4,48,768]{2,1,0:T(8,128)(2,1)S(1)} %copy-done.115), channel_id=1, source_target_pairs={{0,2},{1,3},{2,0},{3,1},{4,6},{5,7},{6,4},{7,5},{8,10},{9,11},{10,... | collective-permute-start | bytes 884744 | tf_op jit(solution)/shard_map/ppermute | solution.py:703
  492.0 40.3 %collective-permute-start.75 = (bf16[768,384]{1,0:T(8,128)(2,1)}, bf16[768,384]{1,0:T(8,128)(2,1)S(1)}, u32[]{:S(2)}, u32[]{:S(2)}) collective-permute-start(bf16[768,384]{1,0:T(8,128)(2,1)} %get-tuple-element.266), channel_id=1, source_target_pairs={{0,1},{1,0},{2,3},{3,2},{4,5},{5,4},{6,7},{7,6},{8,9},{9,8},{10,11... | collective-permute-start | bytes 1769480 | tf_op jit(solution)/shard_map/ppermute | solution.py:703
  500.6 31.9 %collective-permute-start.83 = (bf16[4,48,384]{2,1,0:T(8,128)(2,1)}, bf16[4,48,384]{2,1,0:T(8,128)(2,1)S(1)}, u32[]{:S(2)}, u32[]{:S(2)}) collective-permute-start(bf16[4,48,384]{2,1,0:T(8,128)(2,1)} %get-tuple-element.293), channel_id=1, source_target_pairs={{0,2},{1,3},{2,0},{3,1},{4,6},{5,7},{6,4},{7,5},{8,10},{9,11},{10,... | collective-permute-start | bytes 442376 | tf_op jit(solution)/shard_map/ppermute | solution.py:703
  502.1 53.8 %collective-permute-start.84 = (bf16[4,48,384]{2,1,0:T(8,128)(2,1)}, bf16[4,48,384]{2,1,0:T(8,128)(2,1)S(1)}, u32[]{:S(2)}, u32[]{:S(2)}) collective-permute-start(bf16[4,48,384]{2,1,0:T(8,128)(2,1)} %get-tuple-element.294), channel_id=1, source_target_pairs={{0,4},{1,5},{2,6},{3,7},{4,0},{5,1},{6,2},{7,3},{8,12},{9,13},{10,... | collective-permute-start | bytes 442376 | tf_op jit(solution)/shard_map/ppermute | solution.py:703
  502.2 55.7 %collective-permute-start.85 = (bf16[4,48,384]{2,1,0:T(8,128)(2,1)}, bf16[4,48,384]{2,1,0:T(8,128)(2,1)S(1)}, u32[]{:S(2)}, u32[]{:S(2)}) collective-permute-start(bf16[4,48,384]{2,1,0:T(8,128)(2,1)} %get-tuple-element.295), channel_id=1, source_target_pairs={{0,6},{1,7},{2,4},{3,5},{4,2},{5,3},{6,0},{7,1},{8,14},{9,15},{10,... | collective-permute-start | bytes 442376 | tf_op jit(solution)/shard_map/ppermute | solution.py:703
  504.1 55.3 %collective-permute-start.86 = (bf16[4,48,384]{2,1,0:T(8,128)(2,1)}, bf16[4,48,384]{2,1,0:T(8,128)(2,1)S(1)}, u32[]{:S(2)}, u32[]{:S(2)}) collective-permute-start(bf16[4,48,384]{2,1,0:T(8,128)(2,1)} %get-tuple-element.296), channel_id=1, source_target_pairs={{0,2},{1,3},{2,0},{3,1},{4,6},{5,7},{6,4},{7,5},{8,10},{9,11},{10,... | collective-permute-start | bytes 442376 | tf_op jit(solution)/shard_map/ppermute | solution.py:703
  532.4 47.9 %collective-permute-start.79 = (bf16[768,384]{1,0:T(8,128)(2,1)}, bf16[768,384]{1,0:T(8,128)(2,1)S(1)}, u32[]{:S(2)}, u32[]{:S(2)}) collective-permute-start(bf16[768,384]{1,0:T(8,128)(2,1)} %get-tuple-element.273), channel_id=1, source_target_pairs={{0,1},{1,0},{2,3},{3,2},{4,5},{5,4},{6,7},{7,6},{8,9},{9,8},{10,11... | collective-permute-start | bytes 1769480 | tf_op jit(solution)/shard_map/ppermute | solution.py:703
  579.7 33.2 %collective-permute-start.89 = (bf16[48,384]{1,0:T(8,128)(2,1)S(1)}, bf16[48,384]{1,0:T(8,128)(2,1)S(1)}, u32[]{:S(2)}, u32[]{:S(2)}) collective-permute-start(bf16[48,384]{1,0:T(8,128)(2,1)S(1)} %copy-done.123), channel_id=1, source_target_pairs={{0,8},{1,9},{2,10},{3,11},{4,12},{5,13},{6,14},{7,15},{8,0},{9,1},... | collective-permute-start | bytes 110600 | tf_op jit(solution)/shard_map/ppermute | solution.py:703
  580.3 35.4 %collective-permute-start.90 = (bf16[48,384]{1,0:T(8,128)(2,1)S(1)}, bf16[48,384]{1,0:T(8,128)(2,1)S(1)}, u32[]{:S(2)}, u32[]{:S(2)}) collective-permute-start(bf16[48,384]{1,0:T(8,128)(2,1)S(1)} %copy-done.122), channel_id=1, source_target_pairs={{0,16},{1,17},{2,18},{3,19},{4,20},{5,21},{6,22},{7,23},{8,24},{9,... | collective-permute-start | bytes 110600 | tf_op jit(solution)/shard_map/ppermute | solution.py:703
  (222 other events, 2414.8 us)
